TPU v7x, 256 devices: a whole 4x4x8 slice. The times are simulated.
256 devices in a mesh: market: 32 (over z, y), sub: 8 (over x, core).
Axes of the slice: x: 4, y: 4, z: 8, core: 2. Of those that a mesh axis runs over, the one named last changes fastest.
Arguments:
- buyers: float32 [32768, 512], P(('market', 'sub'))
- sellers: float32 [32768, 512], P(('market', 'sub'))
- eligibility: int32 [32, 32], replicated, may hold values from 0 to 1, as said below
- positives: int32 [32768], P(('market', 'sub')), may hold values from 0 to 32767, as said below
Outputs:
- buyer_grad: float32 [32768, 512], P(('market', 'sub'))
- seller_grad: float32 [32768, 512], P(('market', 'sub'))
- loss: float32 [], replicated
Inputs may be any that keep to these rules, and one draw needn't show every extreme that they name: eligibility[g, g] = 1 for every group; every row has 1 to 16 ones, and some row has exactly 16. positives[i] lies in the same market group as i, and every seller index appears exactly once.
All inputs are finite; a program needn't handle non-finite values.
Results may differ from a plain program's by a relative error of at most 0.0038.
The roundings to bfloat16 on the way count: a program that leaves them out, or rounds other values in their place, can miss the bound.
Values may be sent and summed in bfloat16 or wider, within the bound.
A program may use at most 64 MiB of HBM per device.

v0:
```python
import math

import jax
import jax.numpy as jnp
from jax import lax
from jax.sharding import PartitionSpec as P

neg_fill = -1e30


def merged(part, axis, combine):
    gathered = jax.tree.map(lambda a: lax.all_gather(a, axis), part)

    def take(source):
        return jax.tree.map(lambda a: lax.dynamic_index_in_dim(a, source, 0, False), gathered)

    return lax.fori_loop(
        1, lax.axis_size(axis), lambda source, state: combine(state, take(source)), take(0)
    )


def tile_scores(left, right, factor):
    return (
        lax.dot_general(left, right, (((1,), (1,)), ((), ())), preferred_element_type=jnp.float32)
        * factor
    )


def row_combine(first_part, second_part):
    top = jnp.maximum(first_part[0], second_part[0])
    total = first_part[1] * jnp.exp(first_part[0] - top) + second_part[1] * jnp.exp(
        second_part[0] - top
    )
    return (top, total, first_part[2] + second_part[2])


def col_combine(first_part, second_part):
    top = jnp.maximum(first_part[0], second_part[0])
    total = first_part[1] * jnp.exp(first_part[0] - top) + second_part[1] * jnp.exp(
        second_part[0] - top
    )
    return (top, total)


def coefficient(scores, row_lse, col_lse, is_hit):
    mixed = 0.5 * (jnp.exp(scores - row_lse) + jnp.exp(scores - col_lse)) - jnp.where(
        is_hit, 1.0, 0.0
    )
    return mixed.astype(jnp.bfloat16)


def sweep_groups(stats_step, totals, flags, group_count):

    def outer(state, block_idx):
        outputs = []
        for offset in range(4):
            target = block_idx * 4 + offset
            state, result = stats_step(state, target, flags[target] > 0)
            outputs.append(result)
        stacked = jax.tree.map(lambda *items: jnp.stack(items), *outputs)
        return (state, stacked)

    return lax.scan(outer, totals, jnp.arange(group_count // 4))


def shards(buyers, sellers, eligibility, positives):
    row_count, embed_width = buyers.shape
    sub_count = lax.axis_size("sub")
    group_count = lax.axis_size("market")
    group_rows = row_count * sub_count
    market_pos = lax.axis_index("market")
    sub_pos = lax.axis_index("sub")
    factor = 1.0 / math.sqrt(embed_width)
    local_cols = jnp.arange(row_count, dtype=jnp.int32)
    buyer_half = buyers.astype(jnp.bfloat16)
    seller_half = sellers.astype(jnp.bfloat16)
    group_buyers, group_pos = (
        lax.all_gather(buyer_half, "sub", axis=0, tiled=True),
        lax.all_gather(positives, "sub", axis=0, tiled=True),
    )
    seller_panel = lax.all_gather(seller_half, "market", axis=0, tiled=True)
    own_row = lax.dynamic_index_in_dim(eligibility, market_pos, 0, keepdims=False)

    def panel_block(target):
        return lax.dynamic_slice_in_dim(seller_panel, target * row_count, row_count, 0)

    def stats_step(state, target, is_live):
        row_max, row_sum = state

        def stats_live_branch(unused):
            scores = tile_scores(group_buyers, panel_block(target), factor)
            new_max = jnp.maximum(row_max, jnp.max(scores, axis=1))
            new_sum = row_sum * jnp.exp(row_max - new_max) + jnp.sum(
                jnp.exp(scores - new_max[:, None]), axis=1
            )
            col_top = jnp.max(scores, axis=0)
            col_total = jnp.sum(jnp.exp(scores - col_top[None, :]), axis=0)
            return ((new_max, new_sum), (col_top, col_total))

        def stats_dead_branch(unused):
            return (
                (row_max, row_sum),
                (
                    jnp.full((row_count,), neg_fill, jnp.float32),
                    jnp.zeros((row_count,), jnp.float32),
                ),
            )

        return lax.cond(is_live, stats_live_branch, stats_dead_branch, None)

    start_state = (
        jnp.full((group_rows,), neg_fill, jnp.float32),
        jnp.zeros((group_rows,), jnp.float32),
    )
    (row_max, row_sum), (col_top, col_total) = sweep_groups(
        stats_step, start_state, own_row, group_count
    )
    col_top = col_top.reshape(group_count * row_count)
    col_total = col_total.reshape(group_count * row_count)
    own_scores = tile_scores(group_buyers, seller_half, factor)
    own_ids = (market_pos * sub_count + sub_pos) * row_count + local_cols
    pos_part = jnp.sum(jnp.where(group_pos[:, None] == own_ids[None, :], own_scores, 0.0), axis=1)
    row_max, row_sum, pos_logits = merged((row_max, row_sum, pos_part), "sub", row_combine)
    col_top, col_total = merged((col_top, col_total), "market", col_combine)
    row_lse = row_max + jnp.log(row_sum)
    col_lse = col_top + jnp.log(col_total)
    row_own = lax.dynamic_slice_in_dim(row_lse, sub_pos * row_count, row_count, 0)
    col_own = lax.dynamic_slice_in_dim(col_lse, market_pos * row_count, row_count, 0)
    pos_own = lax.dynamic_slice_in_dim(pos_logits, sub_pos * row_count, row_count, 0)
    local_loss = jnp.sum(row_own) + jnp.sum(col_own) - 2.0 * jnp.sum(pos_own)
    total_loss = lax.psum(local_loss, ("market", "sub"))
    loss = total_loss / (2.0 * group_rows * group_count)

    def grad_step(state, target, is_live):

        def grad_live_branch(acc):
            block = panel_block(target)
            scores = tile_scores(group_buyers, block, factor)
            block_lse = lax.dynamic_slice_in_dim(col_lse, target * row_count, row_count, 0)
            block_ids = (target * sub_count + sub_pos) * row_count + local_cols
            weights_half = coefficient(
                scores,
                row_lse[:, None],
                block_lse[None, :],
                group_pos[:, None] == block_ids[None, :],
            )
            return acc + jnp.dot(weights_half, block, preferred_element_type=jnp.float32)

        return (lax.cond(is_live, grad_live_branch, lambda acc: acc, state), None)

    acc, unused = sweep_groups(
        grad_step,
        jnp.zeros((lax.axis_size("sub") * row_count, embed_width), jnp.float32),
        own_row,
        group_count,
    )
    buyer_grad = lax.psum_scatter(acc, "sub", scatter_dimension=0, tiled=True)
    row_span = lax.axis_size("market") * row_count

    def one_group(offset):

        def one_live_branch(unused):
            block = panel_block(offset)
            scores = tile_scores(group_buyers, block, factor)
            block_lse = lax.dynamic_slice_in_dim(col_lse, offset * row_count, row_count, 0)
            block_ids = (offset * sub_count + sub_pos) * row_count + local_cols
            weights_half = coefficient(
                scores,
                row_lse[:, None],
                block_lse[None, :],
                group_pos[:, None] == block_ids[None, :],
            )
            return lax.dot_general(
                weights_half,
                group_buyers,
                (((0,), (0,)), ((), ())),
                preferred_element_type=jnp.float32,
            )

        def one_dead_branch(unused):
            return jnp.zeros((row_count, embed_width), jnp.float32)

        return lax.cond(own_row[offset] > 0, one_live_branch, one_dead_branch, None)

    pieces = lax.map(one_group, jnp.arange(row_span // row_count))
    seller_grad = lax.psum_scatter(
        pieces.reshape(row_span, embed_width), "market", scatter_dimension=0, tiled=True
    )
    return (buyer_grad, seller_grad, loss)


def solution(mesh):
    return jax.shard_map(
        shards,
        mesh=mesh,
        in_specs=(
            P(("market", "sub"), None),
            P(("market", "sub"), None),
            P(),
            P(("market", "sub")),
        ),
        out_specs=(P(("market", "sub"), None), P(("market", "sub"), None), P()),
        check_vma=False,
    )
```

profile of v0, /device:TPU:2, one launch (start us, length us, event | category | flops | bytes accessed | tf_op | source)
XLA Modules:
  0.0 855.7 jit_solution(17693878719445428025)
XLA Ops:
  7.2 1.6 convert_element_type.100
  8.9 1.6 convert_element_type.99
  10.7 10.1 %all-gather.3 = s32[8,1,128]{2,1,0:T(1,128)S(1)} all-gather(s32[1,1,128]{2,1,0:T(1,128)} %bitcast.146), channel_id=1, replica_groups=mesh['market'=32,'sub'=8] {'sub'}, dimensions={0}, use_global_device_ids=true | all-gather | bytes 4608 | tf_op jit(solution)/shard_map/all_gather | solution.py:79
  20.8 16.8 %all-gather.11.cloned.1.call-done = bf16[1024,512]{1,0:T(8,128)(2,1)} async-done(((bf16[128,512]{1,0:T(8,128)(2,1)}), bf16[1024,512]{1,0:T(8,128)(2,1)}) %all-gather.11.cloned.1.call-update) | async-done | bytes 1048592 | tf_op jit(solution)/shard_map/all_gather | solution.py:78
  37.7 1.7 fusion.105
  39.4 12.8 %all-gather.2 = f32[8192]{0:T(1024)S(1)} all-gather(f32[1024]{0:T(1024)S(1)} %fusion.105), channel_id=4, replica_groups=mesh['market'=32,'sub'=8] {'sub'}, dimensions={0}, use_global_device_ids=true | all-gather | bytes 36864 | tf_op jit(solution)/shard_map/all_gather | solution.py:12
  52.2 72.1 %all-gather.9.cloned.1.call-done = bf16[4096,512]{1,0:T(8,128)(2,1)} async-done(((bf16[128,512]{1,0:T(8,128)(2,1)}), bf16[4096,512]{1,0:T(8,128)(2,1)}) %all-gather.9.cloned.1.call-update) | async-done | bytes 4194320 | tf_op jit(solution)/shard_map/all_gather | solution.py:81
  124.3 76.4 %while.82 = (s32[]{:T(128)}, f32[1024]{0:T(1024)S(1)}, f32[1024]{0:T(1024)S(1)}, f32[8,4,128]{2,1,0:T(4,128)S(1)}, f32[8,4,128]{2,1,0:T(4,128)S(1)}, /*index=5*/...) while((s32[]{:T(128)}, f32[1024]{0:T(1024)S(1)}, ...), condition=%wide.region_25.26_spmd, body=%wide.region_0.25_spmd.sunk | while | flops 540551168 | bytes 9141253 | solution.py:63
  126.8 3.3 conditional.27
  126.9 2.4 fusion.106
  129.3 0.9 exponential_reduce_fusion
  137.1 3.3 conditional.27
  137.1 2.4 fusion.106
  139.5 0.9 exponential_reduce_fusion
  141.1 3.4 conditional.28
  141.1 2.4 fusion.107
  143.6 0.9 exponential_reduce_fusion.2
  146.2 3.4 conditional.30
  146.2 2.5 fusion.109
  148.7 0.9 exponential_reduce_fusion.6
  169.1 3.4 conditional.28
  169.1 2.4 fusion.107
  171.5 0.9 exponential_reduce_fusion.2
  195.4 3.3 conditional.29
  195.4 2.4 fusion.108
  197.8 0.9 exponential_reduce_fusion.4
  200.7 74.2 %all-gather.4 = f32[32,1,4096]{2,1,0:T(1,128)S(1)} all-gather(f32[1,1,4096]{2,1,0:T(1,128)S(1)} %bitcast.140), channel_id=1, replica_groups=mesh['market'=32,'sub'=8] {'market'}, dimensions={0}, use_global_device_ids=true | all-gather | bytes 540672 | tf_op jit(solution)/shard_map/all_gather | solution.py:12
  275.2 46.2 %all-gather.5 = f32[32,1,4096]{2,1,0:T(1,128)S(1)} all-gather(f32[1,1,4096]{2,1,0:T(1,128)S(1)} %bitcast.141), channel_id=1, replica_groups=mesh['market'=32,'sub'=8] {'market'}, dimensions={0}, use_global_device_ids=true | all-gather | bytes 540672 | tf_op jit(solution)/shard_map/all_gather | solution.py:12
  321.7 12.8 %all-gather = f32[8192]{0:T(1024)S(1)} all-gather(f32[1024]{0:T(1024)S(1)} %get-tuple-element.929), channel_id=2, replica_groups=mesh['market'=32,'sub'=8] {'sub'}, dimensions={0}, use_global_device_ids=true | all-gather | bytes 36864 | tf_op jit(solution)/shard_map/all_gather | solution.py:12
  334.5 12.8 %all-gather.1 = f32[8192]{0:T(1024)S(1)} all-gather(f32[1024]{0:T(1024)S(1)} %get-tuple-element.930), channel_id=3, replica_groups=mesh['market'=32,'sub'=8] {'sub'}, dimensions={0}, use_global_device_ids=true | all-gather | bytes 36864 | tf_op jit(solution)/shard_map/all_gather | solution.py:12
  347.3 2.6 while.84
  350.9 48.6 %while.86 = (s32[]{:T(128)}, f32[1024,512]{1,0:T(8,128)S(1)}, s32[8]{0:T(128)S(1)}, s32[32]{0:T(128)S(1)}, bf16[4096,512]{1,0:T(8,128)(2,1)}, /*index=5*/bf16[10...) while((s32[]{:T(128)}, f32[1024,512]{1,0:T(8,128)S(1)}, ...), condition=%wide.region_40.41_spmd.clone.clone, body=%wide.region_31.40_spmd.clone.clone.sunk | while | flops 1080558080 | bytes 22070920 | solution.py:63
  353.5 2.0 conditional.32
  353.6 1.8 convolution_add_fusion
  360.0 2.0 conditional.32
  360.1 1.8 convolution_add_fusion
  362.7 2.0 conditional.33
  362.8 1.8 convolution_add_fusion.1
  365.9 2.0 conditional.35
  366.0 1.9 convolution_add_fusion.3
  380.4 2.0 conditional.33
  380.5 1.8 convolution_add_fusion.1
  396.9 2.0 conditional.34
  397.0 1.8 convolution_add_fusion.2
  399.5 1.4 copy-done.2
  400.9 168.2 %while.85 = (s32[]{:T(128)}, f32[32,128,512]{2,1,0:T(8,128)}, s32[32]{0:T(128)S(1)}, s32[32]{0:T(128)S(1)}, bf16[4096,512]{1,0:T(8,128)(2,1)}, /*index=5*/bf16[1...) while((s32[]{:T(128)}, f32[32,128,512]{2,1,0:T(8,128)}, ...), condition=%wide.region_45.46_spmd.clone, body=%wide.region_42.45_spmd.clone.sunk | while | flops 269615232 | bytes 3027315 | solution.py:185
  404.8 3.1 conditional.31
  406.3 1.6 convolution_bitcast_fusion
  426.6 3.1 conditional.31
  428.0 1.6 convolution_bitcast_fusion
  429.7 0.7 constant_dynamic-update-slice_fusion.2
  434.3 3.1 conditional.31
  435.7 1.6 convolution_bitcast_fusion
  446.7 3.1 conditional.31
  448.2 1.6 convolution_bitcast_fusion
  454.5 0.7 constant_dynamic-update-slice_fusion.2
  496.6 3.1 conditional.31
  498.1 1.6 convolution_bitcast_fusion
  509.1 0.7 constant_dynamic-update-slice_fusion.2
  518.5 0.7 constant_dynamic-update-slice_fusion.2
  560.6 3.1 conditional.31
  562.0 1.6 convolution_bitcast_fusion
  572.3 127.5 %psum.7 = f32[]{:T(128)} all-reduce(f32[]{:T(128)S(6)} %sub.232), channel_id=1, replica_groups=mesh['market'=32,'sub'=8] {'market','sub'}, use_global_device_ids=true, to_apply=%region_50.51 | all-reduce | flops 1 | bytes 8 | tf_op jit(solution)/shard_map/psum | solution.py:131
  700.5 147.5 %reduce-scatter.5.cloned.1.call-done = f32[128,512]{1,0:T(8,128)} async-done(((f32[4096,512]{1,0:T(8,128)}), f32[128,512]{1,0:T(8,128)}) %reduce-scatter.5.cloned.1.call-update) | async-done | bytes 262160 | tf_op jit(solution)/shard_map/reduce_scatter | solution.py:186
  (503 shorter events, 123.9 us)
Async XLA Ops:
  7.2 13.6 %copy-start = (s32[32,32]{1,0:T(8,128)S(1)}, s32[32,32]{1,0:T(8,128)}, u32[]{:S(2)}) copy-start(s32[32,32]{1,0:T(8,128)} %param.34) | copy-start | bytes 12292
  7.2 30.5 %all-gather.11.cloned.1.call-start = ((), (), s32[]{:S(2)}) async-start(), calls=%async_computation.3 | async-start | bytes 1179648 | tf_op jit(solution)/shard_map/all_gather | solution.py:78
  8.9 115.4 %all-gather.9.cloned.1.call-start = ((), (), s32[]{:S(2)}) async-start(), calls=%async_computation.2 | async-start | bytes 4325376 | tf_op jit(solution)/shard_map/all_gather | solution.py:81
  10.6 689.9 %reduce-scatter.3.cloned.1.call-start = ((), (), s32[]{:S(2)}) async-start(), calls=%async_computation.4 | async-start | bytes 2359296 | tf_op jit(solution)/shard_map/reduce_scatter | solution.py:157
  52.2 72.1 %copy-start.3 = (f32[8192]{0:T(1024)}, f32[8192]{0:T(1024)S(1)}, u32[]{:S(2)}) copy-start(f32[8192]{0:T(1024)S(1)} %all-gather.2) | copy-start | bytes 98308
  200.7 149.3 %slice-start = ((f32[8192]{0:T(1024)}), f32[1024]{0:T(1024)S(1)}, s32[]{:S(2)}) async-start(f32[8192]{0:T(1024)} %copy-done.3), calls=%async_computation.6 | async-start | bytes 8192 | tf_op jit(solution)/shard_map/jit(dynamic_index_in_dim)/dynamic_slice | solution.py:15
  200.7 150.2 %copy-start.1 = (bf16[1024,512]{1,0:T(8,128)(2,1)S(1)}, bf16[1024,512]{1,0:T(8,128)(2,1)}, u32[]{:S(2)}) copy-start(bf16[1024,512]{1,0:T(8,128)(2,1)} %get-tuple-element.1708) | copy-start | bytes 3145732
  399.5 1.4 copy-start.2
  400.9 447.1 %reduce-scatter.5.cloned.1.call-start = ((), (), s32[]{:S(2)}) async-start(), calls=%async_computation.5 | async-start | bytes 8650752 | tf_op jit(solution)/shard_map/reduce_scatter | solution.py:186
Sparse Core Ops, SparseCore 0:
  10.4 27.1 all-gather.10
  40.8 83.3 all-gather.8
  401.0 52.4 reduce-scatter.2
  569.3 278.6 reduce-scatter.4
where the time goes:
time: 859 us; the launch traced here: 856 us
  blocking collectives  296 us (34%)
  waiting for transfers between devices  236 us (27%)
  loops' own time  148 us (17%)
  local copies, waits for them, and re-layouts  103 us (12%)
  matrix products  37.2 us (4%)
  between operations  17.6 us (2%)
  other arithmetic  16.4 us (2%)
    all_gather x5, blocking collectives, merged(): gathered = jax.tree.map(lambda a: lax.all_gather(a, axis), part)  159 us
    reduce_scatter x1, waiting for transfers between devices, shards(): lax.psum_scatter(pieces.reshape(row_span, embed_width), 'market', scatter...  147 us
    psum x1, blocking collectives, shards(): total_loss = lax.psum(local_loss, ('market', 'sub'))  127 us
    another operation x1, loops' own time, shards(): pieces = lax.map(one_group, jnp.arange(row_span // row_count))  85.2 us
    all_gather x1, waiting for transfers between devices, shards(): seller_panel = lax.all_gather(seller_half, 'market', axis=0, tiled=True)  72.1 us
    another operation x2, loops' own time, sweep_groups(): return lax.scan(outer, totals, jnp.arange(group_count // 4))  52.1 us
    dynamic_update_slice x32, local copies, waits for them, and re-layouts, shards(): pieces = lax.map(one_group, jnp.arange(row_span // row_count))  23.4 us
    dynamic_slice x32, local copies, waits for them, and re-layouts, one_group(): return lax.cond(own_row[offset] > 0, one_live_branch, one_dead_branch, None)  21.5 us
  transfers between devices with their start and end apart: 4, of which 3 were waited for; matrix products, arithmetic and copies ran while one was open for 9% of the time, Pallas kernels for 0%

commit v1 on v0

--- a/solution.py
+++ b/solution.py
@@ -3,9 +3,678 @@
 import jax
 import jax.numpy as jnp
 from jax import lax
+from jax.experimental import pallas as pl
+from jax.experimental.pallas import tpu as pltpu
 from jax.sharding import PartitionSpec as P
 
 neg_fill = -1e30
+MESH = pl.DeviceIdType.MESH
+NZ, NY, NX, NC = 8, 4, 4, 2
+ROWS = 128
+EMBED = 512
+LOG2E = 1.0 / math.log(2.0)
+SLOTS = 16
+F32 = jnp.float32
+BF16 = jnp.bfloat16
+
+
+def mod(value, size):
+    return lax.rem(value + size, size)
+
+
+def as_row(column, eye):
+    return jnp.sum(jnp.where(eye, column, 0.0), axis=0, keepdims=True)
+
+
+def as_column(row, eye):
+    return jnp.sum(jnp.where(eye, row, 0.0), axis=1, keepdims=True)
+
+
+def kernel(
+    buyers_ref, sellers_ref, elig_ref, pos_ref,
+    bgrad_ref, sgrad_ref, loss_ref,
+    b_all, s_all, bt_all, score, pbuf, qbuf,
+    pos_f, pos_cols, row_stat, col_stat, row_send, row_recv, col_send, col_recv,
+    rowl_send, rowl_recv, coll_send, coll_recv, loss_recv, rl_cols,
+    sib_s, sib_r, z_s, z_r, f0_s, f0_r, f1_s, f1_r, mid, g0_s, g0_r, g1_s, g1_r, seller_t,
+    next_ref, slot_ref, list_ref,
+    send_sem, recv_sem, st_send, st_recv,
+):
+    market = lax.axis_index("market")
+    sub = lax.axis_index("sub")
+    z, y = lax.div(market, NY), lax.rem(market, NY)
+    x, c = lax.div(sub, NC), lax.rem(sub, NC)
+    other = 1 - c
+    row_id = z * NC + c
+    col_id = y * NX + x
+
+    def dev(zz, yy, xx, cc):
+        return (zz * NY + yy, xx * NC + cc)
+
+    def zdev(step):
+        return dev(mod(z + step, NZ), y, x, c)
+
+    def ydev(step):
+        return dev(z, mod(y + step, NY), x, c)
+
+    def xdev(step):
+        return dev(z, y, mod(x + step, NX), c)
+
+    sibling = dev(z, y, x, other)
+
+    def line_dev(place):
+        return dev(lax.div(place, NC), y, x, lax.rem(place, NC))
+
+    def plane_dev(place):
+        return dev(z, lax.div(place, NX), lax.rem(place, NX), c)
+
+    barrier = pltpu.get_barrier_semaphore()
+
+    def greet(step, carry):
+        pl.semaphore_signal(
+            barrier, inc=1, device_id=line_dev(mod(row_id + step, 16)), device_id_type=MESH
+        )
+        pl.semaphore_signal(
+            barrier, inc=1, device_id=plane_dev(mod(col_id + step, 16)), device_id_type=MESH
+        )
+        return carry
+
+    lax.fori_loop(1, 16, greet, 0)
+    b_all[z, c] = buyers_ref[...].astype(BF16)
+    s_all[y, x] = sellers_ref[...].astype(BF16)
+    own_pos = pos_ref[...] - market * (ROWS * NX * NC)
+    pos_f[c] = jnp.broadcast_to(own_pos.astype(F32), (8, ROWS))
+    pl.semaphore_wait(barrier, 30)
+
+    names = {}
+    pending = []
+
+    def sem_of(name):
+        return names.setdefault(name, len(names))
+
+    def send(name, src, dst, device):
+        place = sem_of(name)
+        copy = pltpu.make_async_remote_copy(
+            src_ref=src, dst_ref=dst, send_sem=send_sem.at[place], recv_sem=recv_sem.at[place],
+            device_id=device, device_id_type=MESH,
+        )
+        copy.start()
+        pending.append(copy)
+
+    def arrive(name, dst):
+        place = sem_of(name)
+        pltpu.make_async_remote_copy(
+            src_ref=dst, dst_ref=dst, send_sem=send_sem.at[place], recv_sem=recv_sem.at[place],
+            device_id=sibling, device_id_type=MESH,
+        ).wait_recv()
+
+    def b_at(step, core, lo=0, rows=ROWS):
+        return b_all.at[mod(z + step, NZ), core, pl.ds(lo, rows)]
+
+    def s_at(first_axis, first_step, second_step, lo, rows):
+        if first_axis == "x":
+            return s_all.at[mod(y + second_step, NY), mod(x + first_step, NX), pl.ds(lo, rows)]
+        return s_all.at[mod(y + first_step, NY), mod(x + second_step, NX), pl.ds(lo, rows)]
+
+    halves = (("x", xdev, ydev, 0), ("y", ydev, xdev, 64))
+
+    def send_second(axis, dev2, lo, step1):
+        ref = s_at(axis, step1, 0, lo, 64)
+        for sign in (1, -1):
+            send(("s2", axis, step1, sign), ref, ref, dev2(sign))
+
+    def relay_second(axis, dev2, lo, step1):
+        for sign in (1, -1):
+            arrive(("s2", axis, step1, sign), s_at(axis, step1, -sign, lo, 64))
+            part = lo if sign == 1 else lo + 32
+            ref = s_at(axis, step1, -sign, part, 32)
+            send(("s3", axis, step1, sign), ref, ref, dev2(sign))
+
+    def finish_second(axis, lo, step1):
+        for sign in (1, -1):
+            part = lo if sign == 1 else lo + 32
+            arrive(("s3", axis, step1, sign), s_at(axis, step1, 2, part, 32))
+
+    for sign in (1, -1):
+        send(("b", 1, sign), b_at(0, c), b_at(0, c), zdev(sign))
+    for axis, dev1, dev2, lo in halves:
+        ref = s_at(axis, 0, 0, lo, 64)
+        for sign in (1, -1):
+            send(("s0", axis, sign), ref, ref, dev1(sign))
+    for axis, dev1, dev2, lo in halves:
+        send_second(axis, dev2, lo, 0)
+    send(("pos",), pos_f.at[c], pos_f.at[c], sibling)
+    send(("bs", 0), b_at(0, c), b_at(0, c), sibling)
+
+    own_block = z * NY + y
+
+    def walk_back(i, carry):
+        following, count = carry
+        block = NZ * NY - 1 - i
+        flag = elig_ref[lax.div(block, NY) * NY + y, z * NY + lax.rem(block, NY)]
+        next_ref[block] = following
+        live = jnp.logical_and(flag > 0, block != own_block)
+        return (jnp.where(live, block, following), count + jnp.where(live, 1, 0))
+
+    first, count = lax.fori_loop(0, NZ * NY, walk_back, (own_block, 0))
+
+    def rank(block, seen):
+        flag = elig_ref[lax.div(block, NY) * NY + y, z * NY + lax.rem(block, NY)]
+        live = jnp.logical_and(flag > 0, block != own_block)
+        slot_ref[block] = jnp.where(
+            block == own_block, 0, jnp.where(live, 1 + seen, SLOTS)
+        )
+        return seen + jnp.where(live, 1, 0)
+
+    lax.fori_loop(0, NZ * NY, rank, 0)
+    list_ref[0] = own_block
+
+    def walk(t, block):
+        list_ref[t] = block
+        return next_ref[block]
+
+    lax.fori_loop(1, SLOTS, walk, first)
+
+    for sign in (1, -1):
+        arrive(("b", 1, sign), b_at(-sign, c))
+        send(("b", 2, sign), b_at(-sign, c), b_at(-sign, c), zdev(sign))
+        send(("bs", -sign), b_at(-sign, c), b_at(-sign, c), sibling)
+    for axis, dev1, dev2, lo in halves:
+        for sign in (1, -1):
+            arrive(("s0", axis, sign), s_at(axis, -sign, 0, lo, 64))
+            part = lo if sign == 1 else lo + 32
+            ref = s_at(axis, -sign, 0, part, 32)
+            send(("s1", axis, sign), ref, ref, dev1(sign))
+            send_second(axis, dev2, lo, -sign)
+    for axis, dev1, dev2, lo in halves:
+        relay_second(axis, dev2, lo, 0)
+    for sign in (1, -1):
+        arrive(("b", 2, sign), b_at(-2 * sign, c))
+        send(("b", 3, sign), b_at(-2 * sign, c), b_at(-2 * sign, c), zdev(sign))
+        send(("bs", -2 * sign), b_at(-2 * sign, c), b_at(-2 * sign, c), sibling)
+    for axis, dev1, dev2, lo in halves:
+        for sign in (1, -1):
+            part = lo if sign == 1 else lo + 32
+            arrive(("s1", axis, sign), s_at(axis, 2, 0, part, 32))
+        send_second(axis, dev2, lo, 2)
+    for axis, dev1, dev2, lo in halves:
+        for step1 in (-1, 1):
+            relay_second(axis, dev2, lo, step1)
+    for sign in (1, -1):
+        arrive(("b", 3, sign), b_at(-3 * sign, c))
+        part = 0 if sign == 1 else 64
+        ref = b_at(-3 * sign, c, part, 64)
+        send(("b", 4, sign), ref, ref, zdev(sign))
+        send(("bs", -3 * sign), b_at(-3 * sign, c), b_at(-3 * sign, c), sibling)
+    for axis, dev1, dev2, lo in halves:
+        relay_second(axis, dev2, lo, 2)
+    for sign in (1, -1):
+        part = 0 if sign == 1 else 64
+        arrive(("b", 4, sign), b_at(4, c, part, 64))
+    send(("bs", 4), b_at(4, c), b_at(4, c), sibling)
+    for axis, dev1, dev2, lo in halves:
+        for step1 in (0, -1, 1, 2):
+            finish_second(axis, lo, step1)
+    arrive(("pos",), pos_f.at[other])
+    for step in (0, 1, -1, 2, -2, 3, -3, 4):
+        arrive(("bs", step), b_at(step, other))
+
+    eye = lax.broadcasted_iota(jnp.int32, (ROWS, ROWS), 0) == lax.broadcasted_iota(
+        jnp.int32, (ROWS, ROWS), 1
+    )
+    unit = LOG2E / math.sqrt(EMBED)
+
+    def transpose_buyers(zz, carry):
+        bt_all[zz] = b_all[zz].reshape(NC * ROWS, EMBED).T
+        return carry
+
+    lax.fori_loop(0, NZ, transpose_buyers, 0)
+    for core in range(NC):
+        pos_cols[core * ROWS : (core + 1) * ROWS, :] = jnp.broadcast_to(
+            as_column(pos_f[core, 0:1, :], eye), (ROWS, ROWS)
+        )
+
+    def hits(xx):
+        lane = lax.broadcasted_iota(jnp.int32, (NC * ROWS, ROWS), 1) + (xx * NC + c) * ROWS
+        return pos_cols[...] == lane.astype(F32)
+
+    row_stat[SLOTS] = jnp.zeros(row_stat.shape[1:], F32)
+    col_stat[SLOTS] = jnp.zeros(col_stat.shape[1:], F32)
+    for core in range(NC):
+        row_stat[SLOTS, core, 0:1, :] = jnp.full((1, ROWS), neg_fill, F32)
+    for xx in range(NX):
+        col_stat[SLOTS, xx, 0:1, :] = jnp.full((1, ROWS), neg_fill, F32)
+
+    def first_pass(t, carry):
+        block = list_ref[t]
+        left = b_all[lax.div(block, NY)].reshape(NC * ROWS, EMBED)
+        right = s_all[lax.rem(block, NY)].reshape(NX * ROWS, EMBED)
+        tile = (
+            lax.dot_general(left, right, (((1,), (1,)), ((), ())), preferred_element_type=F32)
+            * unit
+        )
+        score[t] = tile
+        row_top = jnp.max(tile, axis=1, keepdims=True)
+        row_sum = jnp.sum(jnp.exp2(tile - row_top), axis=1, keepdims=True)
+        col_top = jnp.max(tile, axis=0, keepdims=True)
+        col_sum = jnp.sum(jnp.exp2(tile - col_top), axis=0, keepdims=True)
+        for core in range(NC):
+            span = slice(core * ROWS, (core + 1) * ROWS)
+            row_stat[t, core, 0:1, :] = as_row(row_top[span], eye)
+            row_stat[t, core, 1:2, :] = as_row(row_sum[span], eye)
+        for xx in range(NX):
+            span = slice(xx * ROWS, (xx + 1) * ROWS)
+            col_stat[t, xx, 0:1, :] = col_top[:, span]
+            col_stat[t, xx, 1:2, :] = col_sum[:, span]
+        return carry
+
+    lax.fori_loop(0, SLOTS, first_pass, 0)
+    matched = jnp.zeros((NC * ROWS, 1), F32)
+    for xx in range(NX):
+        matched = matched + jnp.sum(
+            jnp.where(hits(xx), score[0, :, xx * ROWS : (xx + 1) * ROWS], 0.0),
+            axis=1, keepdims=True,
+        )
+
+    def merge(tops, sums):
+        top = tops[0]
+        for item in tops[1:]:
+            top = jnp.maximum(top, item)
+        total = jnp.zeros_like(top)
+        for item, amount in zip(tops, sums):
+            total = total + amount * jnp.exp2(item - top)
+        return top, total
+
+    row_send[...] = jnp.zeros(row_send.shape, F32)
+    col_send[...] = jnp.zeros(col_send.shape, F32)
+    for core in range(NC):
+        row_send[z * NC + core, 2:3, :] = as_row(matched[core * ROWS : (core + 1) * ROWS], eye)
+
+    def merge_rows(zz, carry):
+        slots = [slot_ref[zz * NY + yy] for yy in range(NY)]
+        for core in range(NC):
+            top, total = merge(
+                [row_stat[s, core, 0:1, :] for s in slots], [row_stat[s, core, 1:2, :] for s in slots]
+            )
+            row_send[zz * NC + core, 0:1, :] = top
+            row_send[zz * NC + core, 1:2, :] = total
+        return carry
+
+    lax.fori_loop(0, NZ, merge_rows, 0)
+
+    def merge_cols(yy, carry):
+        slots = [slot_ref[zz * NY + yy] for zz in range(NZ)]
+        for xx in range(NX):
+            top, total = merge(
+                [col_stat[s, xx, 0:1, :] for s in slots], [col_stat[s, xx, 1:2, :] for s in slots]
+            )
+            col_send[yy * NX + xx, 0:1, :] = top
+            col_send[yy * NX + xx, 1:2, :] = total
+        return carry
+
+    lax.fori_loop(0, NY, merge_cols, 0)
+
+    def small(kind, src, dst, step, device):
+        return pltpu.make_async_remote_copy(
+            src_ref=src, dst_ref=dst, send_sem=st_send.at[kind, step],
+            recv_sem=st_recv.at[kind, step], device_id=device, device_id_type=MESH,
+        )
+
+    def scatter(step, carry):
+        to = mod(row_id + step, 16)
+        small(0, row_send.at[to], row_recv.at[row_id], step, line_dev(to)).start()
+        to = mod(col_id + step, 16)
+        small(1, col_send.at[to], col_recv.at[col_id], step, plane_dev(to)).start()
+        return carry
+
+    def scattered(step, carry):
+        origin = mod(row_id - step, 16)
+        small(0, row_send.at[origin], row_recv.at[origin], step, sibling).wait()
+        origin = mod(col_id - step, 16)
+        small(1, col_send.at[origin], col_recv.at[origin], step, sibling).wait()
+        return carry
+
+    lax.fori_loop(1, 16, scatter, 0)
+    row_recv[row_id] = row_send[row_id]
+    col_recv[col_id] = col_send[col_id]
+    lax.fori_loop(1, 16, scattered, 0)
+
+    def own_lse(recv):
+        top, total = merge(
+            [recv[i, 0:1, :] for i in range(16)], [recv[i, 1:2, :] for i in range(16)]
+        )
+        return top + jnp.log2(total)
+
+    own_row, own_col = own_lse(row_recv), own_lse(col_recv)
+    own_match = row_recv[0, 2:3, :]
+    for i in range(1, 16):
+        own_match = own_match + row_recv[i, 2:3, :]
+    terms = jnp.sum(own_row + own_col - 2.0 * own_match, axis=1, keepdims=True)
+    rowl_send[0:1, :] = own_row
+    rowl_send[1:8, :] = jnp.broadcast_to(terms, (7, ROWS))
+    coll_send[...] = jnp.broadcast_to(own_col, (8, ROWS))
+
+    def spread(step, carry):
+        to = mod(row_id + step, 16)
+        small(2, rowl_send, rowl_recv.at[row_id], step, line_dev(to)).start()
+        to = mod(col_id + step, 16)
+        small(3, coll_send, coll_recv.at[col_id], step, plane_dev(to)).start()
+        return carry
+
+    def spreaded(step, carry):
+        small(2, rowl_send, rowl_recv.at[mod(row_id - step, 16)], step, sibling).wait()
+        small(3, coll_send, coll_recv.at[mod(col_id - step, 16)], step, sibling).wait()
+        return carry
+
+    lax.fori_loop(1, 16, spread, 0)
+    rowl_recv[row_id] = rowl_send[...]
+    coll_recv[col_id] = coll_send[...]
+    lax.fori_loop(1, 16, spreaded, 0)
+
+    line_terms = rowl_recv[0, 1:2, :]
+    for i in range(1, 16):
+        line_terms = line_terms + rowl_recv[i, 1:2, :]
+    loss_recv[col_id] = jnp.broadcast_to(line_terms, (8, ROWS))
+
+    def tell(step, carry):
+        to = mod(col_id + step, 16)
+        small(4, loss_recv.at[col_id], loss_recv.at[col_id], step, plane_dev(to)).start()
+        return carry
+
+    lax.fori_loop(1, 16, tell, 0)
+
+    def spread_rows(zz, carry):
+        for core in range(NC):
+            rl_cols[zz, core * ROWS : (core + 1) * ROWS, :] = jnp.broadcast_to(
+                as_column(rowl_recv[zz * NC + core, 0:1, :], eye) + 1.0, (ROWS, ROWS)
+            )
+        return carry
+
+    lax.fori_loop(0, NZ, spread_rows, 0)
+
+    def second_pass(t, own):
+        block = list_ref[t]
+        zz, yy = lax.div(block, NY), lax.rem(block, NY)
+        row_lse = rl_cols[zz]
+        parts = []
+        for xx in range(NX):
+            tile = score[t, :, xx * ROWS : (xx + 1) * ROWS]
+            col_lse = coll_recv[yy * NX + xx, 0:1, :] + 1.0
+            mixed = jnp.exp2(tile - row_lse) + jnp.exp2(tile - col_lse)
+            if own:
+                mixed = mixed - jnp.where(hits(xx), 1.0, 0.0)
+            parts.append(mixed.astype(BF16))
+        weights = jnp.concatenate(parts, axis=1)
+        right = s_all[yy].reshape(NX * ROWS, EMBED)
+        term = jnp.dot(weights, right, preferred_element_type=F32)
+        for core in range(NC):
+            pbuf[t, core] = term[core * ROWS : (core + 1) * ROWS]
+        term = jnp.dot(bt_all[zz], weights, preferred_element_type=F32)
+        for xx in range(NX):
+            qbuf[t, xx] = term[:, xx * ROWS : (xx + 1) * ROWS]
+
+    second_pass(0, True)
+
+    def other_blocks(t, carry):
+        second_pass(t, False)
+        return carry
+
+    lax.fori_loop(1, SLOTS, other_blocks, 0)
+    pbuf[SLOTS] = jnp.zeros(pbuf.shape[1:], F32)
+    qbuf[SLOTS] = jnp.zeros(qbuf.shape[1:], F32)
+
+    step_rows = 32
+
+    def by_rows(lo, rows, body):
+        def at(i, carry):
+            body(pl.multiple_of(lo + i * step_rows, step_rows))
+            return carry
+
+        lax.fori_loop(0, rows // step_rows, at, 0)
+
+    def p_sum(zz, core, at):
+        total = None
+        for yy in range(NY):
+            term = pbuf[slot_ref[zz * NY + yy], core, pl.ds(at, step_rows), :]
+            total = term if total is None else total + term
+        return total
+
+    def q_sum(yy, xx, at):
+        total = None
+        for zz in range(NZ):
+            term = qbuf[slot_ref[zz * NY + yy], xx, pl.ds(at, step_rows), :]
+            total = term if total is None else total + term
+        return total
+
+    order = (4, 3, -3, 2, -2, 1, -1, 0)
+    for place, step in enumerate(order):
+        def fill(at, place=place, step=step):
+            sib_s[place, pl.ds(at, step_rows), :] = p_sum(mod(z + step, NZ), other, at).astype(BF16)
+
+        by_rows(0, ROWS, fill)
+        send(("gs", place), sib_s.at[place], sib_r.at[place], sibling)
+
+    grads = ((0, "y", ydev, xdev, 0), (1, "x", xdev, ydev, 256))
+
+    def q_at(axis, step, lane, at):
+        if axis == "y":
+            return q_sum(mod(y + step, NY), lane, at)
+        return q_sum(lane, mod(x + step, NX), at)
+
+    for h, axis, dev1, dev2, base in grads:
+        for d, sign in enumerate((1, -1)):
+            for lane in range(4):
+                def fill(at, h=h, axis=axis, d=d, lane=lane, base=base):
+                    f0_s[h, d, lane, pl.ds(at, step_rows), :] = q_at(
+                        axis, 2, lane, base + d * 128 + at
+                    ).astype(BF16)
+
+                by_rows(0, 128, fill)
+            send(("f0", h, sign), f0_s.at[h, d], f0_r.at[h, d], dev1(sign))
+
+    def z_value(place, step, at):
+        return p_sum(mod(z + step, NZ), c, at) + sib_r[place, pl.ds(at, step_rows), :].astype(F32)
+
+    def z_send(place, step, d, sign, hop, lo, rows):
+        def fill(at):
+            value = z_value(place, step, at)
+            z_s[d, hop, pl.ds(at, step_rows), :] = value.astype(BF16)
+
+        def fill_more(at):
+            value = z_value(place, step, at)
+            value = value + z_r[d, hop - 1, pl.ds(at, step_rows), :].astype(F32)
+            z_s[d, hop, pl.ds(at, step_rows), :] = value.astype(BF16)
+
+        if hop == 0:
+            by_rows(lo, rows, fill)
+        elif hop == 1:
+            first_lo = d * 64
+            arrive(("gz", 0, sign), z_r.at[d, 0, pl.ds(first_lo, 64)])
+            by_rows(first_lo, 64, fill_more)
+            by_rows(64 - first_lo, 64, fill)
+        else:
+            arrive(("gz", hop - 1, sign), z_r.at[d, hop - 1])
+            by_rows(0, ROWS, fill_more)
+        ref = z_s.at[d, hop, pl.ds(lo, rows)]
+        send(("gz", hop, sign), ref, z_r.at[d, hop, pl.ds(lo, rows)], zdev(sign))
+
+    arrive(("gs", 0), sib_r.at[0])
+    z_send(0, 4, 0, 1, 0, 0, 64)
+    z_send(0, 4, 1, -1, 0, 64, 64)
+
+    for h, axis, dev1, dev2, base in grads:
+        for d, sign in enumerate((1, -1)):
+            for lane in range(4):
+                def fill(at, h=h, axis=axis, d=d, sign=sign, lane=lane, base=base):
+                    f1_s[h, d, lane, pl.ds(at, step_rows), :] = q_at(
+                        axis, sign, lane, base + at
+                    ).astype(BF16)
+
+                def fill_more(at, h=h, axis=axis, d=d, sign=sign, lane=lane, base=base):
+                    value = q_at(axis, sign, lane, base + d * 128 + at)
+                    value = value + f0_r[h, d, lane, pl.ds(at, step_rows), :].astype(F32)
+                    f1_s[h, d, lane, pl.ds(d * 128 + at, step_rows), :] = value.astype(BF16)
+
+                by_rows(128 - d * 128, 128, fill)
+                if lane == 0:
+                    arrive(("f0", h, sign), f0_r.at[h, d])
+                by_rows(0, 128, fill_more)
+            send(("f1", h, sign), f1_s.at[h, d], f1_r.at[h, d], dev1(sign))
+
+    arrive(("gs", 1), sib_r.at[1])
+    z_send(1, 3, 0, 1, 1, 0, ROWS)
+    arrive(("gs", 2), sib_r.at[2])
+    z_send(2, -3, 1, -1, 1, 0, ROWS)
+
+    for h, axis, dev1, dev2, base in grads:
+        for lane in range(4):
+            def own_fill(at, h=h, axis=axis, lane=lane, base=base):
+                mid[h, lane, pl.ds(at, step_rows), :] = q_at(axis, 0, lane, base + at)
+
+            by_rows(0, 256, own_fill)
+    arrive(("gs", 3), sib_r.at[3])
+    z_send(3, 2, 0, 1, 2, 0, ROWS)
+    arrive(("gs", 4), sib_r.at[4])
+    z_send(4, -2, 1, -1, 2, 0, ROWS)
+
+    for h, axis, dev1, dev2, base in grads:
+        for d, sign in enumerate((1, -1)):
+            arrive(("f1", h, sign), f1_r.at[h, d])
+        for lane in range(4):
+            def own_add(at, h=h, lane=lane):
+                span = pl.ds(at, step_rows)
+                mid[h, lane, span, :] = (
+                    mid[h, lane, span, :]
+                    + f1_r[h, 0, lane, span, :].astype(F32)
+                    + f1_r[h, 1, lane, span, :].astype(F32)
+                )
+
+            by_rows(0, 256, own_add)
+        place = x if axis == "y" else y
+        far = mod(place + 2, 4)
+        for d, sign in enumerate((1, -1)):
+            g0_s[h, d] = mid[h, far, d * 128 : (d + 1) * 128, :].astype(BF16)
+            send(("g0", h, sign), g0_s.at[h, d], g0_r.at[h, d], dev2(sign))
+    for h, axis, dev1, dev2, base in grads:
+        place = x if axis == "y" else y
+        for d, sign in enumerate((1, -1)):
+            near = mod(place + sign, 4)
+            arrive(("g0", h, sign), g0_r.at[h, d])
+            own_lo = 128 - d * 128
+            g1_s[h, d, own_lo : own_lo + 128, :] = mid[
+                h, near, own_lo : own_lo + 128, :
+            ].astype(BF16)
+            g1_s[h, d, d * 128 : (d + 1) * 128, :] = (
+                mid[h, near, d * 128 : (d + 1) * 128, :] + g0_r[h, d].astype(F32)
+            ).astype(BF16)
+            send(("g1", h, sign), g1_s.at[h, d], g1_r.at[h, d], dev2(sign))
+
+    arrive(("gs", 5), sib_r.at[5])
+    z_send(5, 1, 0, 1, 3, 0, ROWS)
+    arrive(("gs", 6), sib_r.at[6])
+    z_send(6, -1, 1, -1, 3, 0, ROWS)
+
+    for h, axis, dev1, dev2, base in grads:
+        place = x if axis == "y" else y
+        for d, sign in enumerate((1, -1)):
+            arrive(("g1", h, sign), g1_r.at[h, d])
+        seller_t[h * 256 : (h + 1) * 256, :] = (
+            mid[h, place] + g1_r[h, 0].astype(F32) + g1_r[h, 1].astype(F32)
+        )
+    sgrad_ref[...] = seller_t[...].T
+
+    arrive(("gs", 7), sib_r.at[7])
+    for d, sign in enumerate((1, -1)):
+        arrive(("gz", 3, sign), z_r.at[d, 3])
+
+    def finish(at):
+        span = pl.ds(at, step_rows)
+        bgrad_ref[span, :] = (
+            z_value(7, 0, at) + z_r[0, 3, span, :].astype(F32) + z_r[1, 3, span, :].astype(F32)
+        )
+
+    by_rows(0, ROWS, finish)
+
+    def told(step, carry):
+        small(
+            4, loss_recv.at[col_id], loss_recv.at[mod(col_id - step, 16)], step, sibling
+        ).wait()
+        return carry
+
+    lax.fori_loop(1, 16, told, 0)
+    total = loss_recv[0, 0:1, :]
+    for i in range(1, 16):
+        total = total + loss_recv[i, 0:1, :]
+    loss_ref[...] = total * (math.log(2.0) / (2.0 * ROWS * NZ * NY * NX * NC))
+    for copy in pending:
+        copy.wait_send()
+
+
+def vmem(shape, dtype):
+    return pltpu.VMEM(shape, dtype)
+
+
+def fast(buyers, sellers, eligibility, positives):
+    scratch = [
+        vmem((NZ, NC, ROWS, EMBED), BF16),
+        vmem((NY, NX, ROWS, EMBED), BF16),
+        vmem((NZ, EMBED, NC * ROWS), BF16),
+        vmem((SLOTS, NC * ROWS, NX * ROWS), F32),
+        vmem((SLOTS + 1, NC, ROWS, EMBED), F32),
+        vmem((SLOTS + 1, NX, EMBED, ROWS), F32),
+        vmem((NC, 8, ROWS), F32),
+        vmem((NC * ROWS, ROWS), F32),
+        vmem((SLOTS + 1, NC, 8, ROWS), F32),
+        vmem((SLOTS + 1, NX, 8, ROWS), F32),
+        vmem((16, 8, ROWS), F32),
+        vmem((16, 8, ROWS), F32),
+        vmem((16, 8, ROWS), F32),
+        vmem((16, 8, ROWS), F32),
+        vmem((8, ROWS), F32),
+        vmem((16, 8, ROWS), F32),
+        vmem((8, ROWS), F32),
+        vmem((16, 8, ROWS), F32),
+        vmem((16, 8, ROWS), F32),
+        vmem((NZ, NC * ROWS, ROWS), F32),
+        vmem((NZ, ROWS, EMBED), BF16),
+        vmem((NZ, ROWS, EMBED), BF16),
+        vmem((2, 4, ROWS, EMBED), BF16),
+        vmem((2, 4, ROWS, EMBED), BF16),
+        vmem((2, 2, 4, 128, ROWS), BF16),
+        vmem((2, 2, 4, 128, ROWS), BF16),
+        vmem((2, 2, 4, 256, ROWS), BF16),
+        vmem((2, 2, 4, 256, ROWS), BF16),
+        vmem((2, 4, 256, ROWS), F32),
+        vmem((2, 2, 128, ROWS), BF16),
+        vmem((2, 2, 128, ROWS), BF16),
+        vmem((2, 2, 256, ROWS), BF16),
+        vmem((2, 2, 256, ROWS), BF16),
+        vmem((EMBED, ROWS), F32),
+        pltpu.SMEM((NZ * NY,), jnp.int32),
+        pltpu.SMEM((NZ * NY,), jnp.int32),
+        pltpu.SMEM((SLOTS,), jnp.int32),
+        pltpu.SemaphoreType.DMA((96,)),
+        pltpu.SemaphoreType.DMA((96,)),
+        pltpu.SemaphoreType.DMA((5, 16)),
+        pltpu.SemaphoreType.DMA((5, 16)),
+    ]
+    in_vmem = pl.BlockSpec(memory_space=pltpu.VMEM)
+    buyer_grad, seller_grad, loss = pl.pallas_call(
+        kernel,
+        out_shape=(
+            jax.ShapeDtypeStruct((ROWS, EMBED), F32),
+            jax.ShapeDtypeStruct((ROWS, EMBED), F32),
+            jax.ShapeDtypeStruct((1, ROWS), F32),
+        ),
+        in_specs=[in_vmem, in_vmem, pl.BlockSpec(memory_space=pltpu.SMEM), in_vmem],
+        out_specs=(in_vmem, in_vmem, in_vmem),
+        scratch_shapes=scratch,
+        compiler_params=pltpu.CompilerParams(
+            collective_id=0, has_side_effects=True, vmem_limit_bytes=60 * 1024 * 1024
+        ),
+        name="two_tower",
+    )(buyers, sellers, eligibility, positives.reshape(1, ROWS))
+    return (buyer_grad, seller_grad, loss[0, 0])
 
 
 def merged(part, axis, combine):
@@ -63,7 +732,7 @@
     return lax.scan(outer, totals, jnp.arange(group_count // 4))
 
 
-def shards(buyers, sellers, eligibility, positives):
+def general(buyers, sellers, eligibility, positives):
     row_count, embed_width = buyers.shape
     sub_count = lax.axis_size("sub")
     group_count = lax.axis_size("market")
@@ -189,6 +858,12 @@
     return (buyer_grad, seller_grad, loss)
 
 
+def shards(buyers, sellers, eligibility, positives):
+    blocks = (eligibility > 0).astype(jnp.int32).reshape(NZ, NY, NZ, NY)
+    busiest = jnp.max(jnp.sum(blocks, axis=(0, 3)))
+    return lax.cond(busiest <= SLOTS, fast, general, buyers, sellers, eligibility, positives)
+
+
 def solution(mesh):
     return jax.shard_map(
         shards,

time: 859 us -> 109 us (0.13)
  blocking collectives: 296 us -> 0 us
  waiting for transfers between devices: 236 us -> 0 us
  loops' own time: 148 us -> 0.82 us
  local copies, waits for them, and re-layouts: 103 us -> 3.43 us
  Pallas kernels: 0 us -> 86.3 us
  matrix products: 37.2 us -> 0 us
  other arithmetic: 16.4 us -> 1.52 us
    all_gather x6 -> x0, blocking collectives: 169 us -> none  [the longest x5 159 us: merged(): gathered = jax.tree.map(lambda a: lax.all_gather(a, axis), part)]
    reduce_scatter x2 -> x0, waiting for transfers between devices: 147 us -> none  [the longest x1 147 us: shards(): lax.psum_scatter(pieces.reshape(row_span, embed_width), 'market', scatter...]
    another operation x101 -> x1, loops' own time: 148 us -> 0.82 us  [shards(): lax.cond(busiest <= SLOTS, fast, general, buyers, sellers, eligibility, p...]
    psum x1 -> x0, blocking collectives: 127 us -> none  [shards(): total_loss = lax.psum(local_loss, ('market', 'sub'))]
    all_gather x2 -> x0, waiting for transfers between devices: 88.9 us -> none  [the longest x1 72.1 us: shards(): seller_panel = lax.all_gather(seller_half, 'market', axis=0, tiled=True)]
    pallas_call x0 -> x1, Pallas kernels: none -> 86.3 us  [fast(): pl.pallas_call(kernel, out_shape=(jax.ShapeDtypeStruct((ROWS, EMBED), F32...]
    dynamic_slice x159 -> x0, local copies, waits for them, and re-layouts: 62.2 us -> none  [the longest x32 21.5 us: one_group(): return lax.cond(own_row[offset] > 0, one_live_branch, one_dead_branch, None)]
    dot_general x19 -> x0, matrix products: 37.2 us -> none  [the longest x7 16.3 us: tile_scores(): lax.dot_general(left, right, (((1,), (1,)), ((), ())), preferred_element_...]
  transfers between devices with their start and end apart: 4 -> 0, of which waited for: 3 -> 0; matrix products, arithmetic and copies ran while one was open for 9% -> 0% of each run, Pallas kernels for 0% -> 0%
where the time goes in v1:
time: 109 us; the launch traced here: 108 us
  Pallas kernels  86.3 us (79%)
  between operations  15.8 us (14%)
  local copies, waits for them, and re-layouts  3.43 us (3%)
  other arithmetic  1.52 us (1%)
    pallas_call x1, Pallas kernels, fast(): pl.pallas_call(kernel, out_shape=(jax.ShapeDtypeStruct((ROWS, EMBED), F32...  86.3 us
    unnamed x2, local copies, waits for them, and re-layouts  3.34 us

profile of v1, /device:TPU:2, one launch (start us, length us, event | category | flops | bytes accessed | tf_op | source)
XLA Modules:
  0.0 107.9 jit_solution(3278575990204020693)
XLA Ops:
  7.2 0.7 compare_convert_fusion
  7.9 0.1 reshape.109
  8.0 0.2 reduce_sum.117
  8.1 0.6 reduce_max.81
  9.4 87.2 %conditional.10 = (f32[128,512]{1,0:T(8,128)}, f32[128,512]{1,0:T(8,128)}, f32[]{:T(128)}) conditional(s32[]{:T(128)} %convert_element_type.103, (s32[32,32]{1,0:T(8,128)}, f32[128,512]{1,0:T(8,128)}, f32[128,512]{1,0:T(8,128)}, s32[128]{0:T(128)}) %tuple.170, (s32[128]{0:T(128)}, f32[128,512]{1,0:T(8,128)}, f32[128,512]{1,0:T(8,128)}, ...), branch_computations={%region_2.54_spmd, %region_54.55_spmd} | conditional | flops 2025633920 | bytes 104454040 | solution.py:864
  9.6 86.3 %two_tower.1 = (f32[128,512]{1,0:T(8,128)}, f32[128,512]{1,0:T(8,128)}, f32[1,128]{1,0:T(1,128)}) custom-call(f32[128,512]{1,0:T(8,128)} %get-tuple-element.946.buyers_ref, f32[128,512]{1,0:T(8,128)} %get-tuple-element.947.sellers_ref, s32[32,32]{1,0:T(8,128)} %get-tuple-element.948.elig_ref, s32[1,128]{1,0:T(1,128)} %bitcast.150), custom_call_target="tpu_custom_call" | custom-call | tf_op jit(solution)/shard_map/cond/branch_1_fun/two_tower/pallas_call | solution.py:662
  96.6 1.7 %copy.121 = f32[128,512]{1,0:T(8,128)} copy(f32[128,512]{1,0:T(8,128)} %get-tuple-element.1726) | data formatting | bytes 524288
  98.3 1.7 %copy.122 = f32[128,512]{1,0:T(8,128)} copy(f32[128,512]{1,0:T(8,128)} %get-tuple-element.1727) | data formatting | bytes 524288

commit v2 on v0

--- a/solution.py
+++ b/solution.py
@@ -1,15 +1,725 @@
+import functools
 import math
 
 import jax
 import jax.numpy as jnp
 from jax import lax
+from jax.experimental import pallas as pl
+from jax.experimental.pallas import tpu as pltpu
 from jax.sharding import PartitionSpec as P
 
 neg_fill = -1e30
+MESH = pl.DeviceIdType.MESH
+NZ, NY, NX, NC = 8, 4, 4, 2
+ROWS = 128
+EMBED = 512
+LOG2E = 1.0 / math.log(2.0)
+SLOTS = 14
+F32 = jnp.float32
+BF16 = jnp.bfloat16
+
+
+GATHER_ORDER = (
+    ("b", 0, -1, 0), ("s0", 0, -1), ("bs", 0), ("b", 0, 1, 0), ("s0", 0, 1), ("s0", 1, 1), ("s2", 1, 0, 1),
+    ("s0", 1, -1), ("b", 0, -1, 2), ("b", 0, 1, 1), ("b", 0, -1, 1), ("b", 0, 1, 2), ("s2", 0, 0, -1),
+    ("s2", 0, 0, 1), ("s2", 1, 0, -1), ("b", 1, -1, 0), ("s2", 0, 1, 1), ("b", 1, 1, 0), ("s2", 1, -1, 1),
+    ("s2", 0, 1, -1), ("s1", 0, -1), ("s1", 1, -1), ("b", 1, -1, 1), ("b", 1, 1, 1), ("b", 1, -1, 2),
+    ("s1", 1, 1), ("s1", 0, 1), ("b", 1, 1, 2), ("s3", 0, 0, -1), ("s2", 1, 1, -1), ("s2", 1, 1, 1),
+    ("s2", 1, -1, -1), ("s2", 0, -1, 1), ("s3", 0, 1, 1), ("b", 2, -1, 0), ("b", 2, 1, 1), ("s2", 0, -1, -1),
+    ("b", 2, -1, 1), ("b", 2, 1, 0), ("s2", 1, 2, 1), ("b", 2, -1, 2), ("s2", 1, 2, -1), ("b", 2, 1, 2),
+    ("s2", 0, 2, -1), ("s4", 0, 0, -1), ("bs", 2), ("s2", 0, 2, 1), ("bs", 1), ("bs", -2), ("s3", 1, 0, 1),
+    ("s3", 1, -1, 1), ("s4", 0, 1, 1), ("b", 3, 1, 1), ("b", 3, -1, 0), ("s3", 1, 1, -1), ("b", 3, 1, 0),
+    ("b", 3, -1, 1), ("s3", 0, -1, 1), ("s3", 1, -1, -1), ("s3", 0, 1, -1), ("s3", 1, 0, -1), ("s3", 1, 1, 1),
+    ("bs", -1), ("s3", 0, 0, 1), ("s3", 1, 2, 1), ("s3", 0, -1, -1), ("bs", 3), ("s3", 1, 2, -1),
+    ("s3", 0, 2, -1), ("s3", 0, 2, 1), ("bs", -3), ("bs", 4), ("s4", 1, 0, 1), ("s4", 1, 1, -1),
+    ("s4", 0, -1, 1), ("s4", 1, 0, -1), ("s4", 0, -1, -1), ("s4", 1, -1, -1), ("s4", 1, -1, 1),
+    ("s4", 1, 1, 1), ("s4", 0, 2, 1), ("s4", 0, 1, -1), ("s4", 0, 0, 1), ("s4", 0, 2, -1), ("s4", 1, 2, 1),
+    ("s4", 1, 2, -1),
+)
+RETURN_ORDER = (
+    ("f0", 1, 1, 0), ("sib", 0), ("f0", 1, 0, 0), ("f0", 0, 0, 0), ("f0", 0, 1, 2), ("sib", 4),
+    ("f0", 1, 1, 2), ("f0", 1, 0, 1), ("f0", 0, 1, 0), ("fa", 1, 0, 2), ("sib", 2), ("f0", 0, 0, 1),
+    ("f0", 1, 0, 2), ("loss", 0), ("f0", 1, 1, 1), ("fa", 0, 1, 0), ("sib", 1), ("z", 0, 0, 0),
+    ("z", 1, 0, 3), ("sib", 7), ("z", 0, 0, 1), ("fa", 1, 1, 0), ("f0", 0, 0, 2), ("f0", 0, 1, 1),
+    ("z", 1, 0, 2), ("sib", 5), ("z", 0, 1, 3), ("sib", 3), ("fb", 0, 0, 0), ("z", 1, 1, 0), ("fa", 0, 0, 0),
+    ("fb", 1, 1, 0), ("fb", 1, 0, 0), ("fa", 1, 1, 1), ("loss", 1), ("fa", 0, 1, 1), ("z", 0, 1, 2),
+    ("z", 1, 1, 1), ("fb", 0, 1, 0), ("fa", 1, 0, 0), ("z", 1, 1, 3), ("z", 0, 1, 0), ("fa", 1, 1, 2),
+    ("fa", 0, 0, 1), ("fa", 1, 0, 1), ("z", 0, 1, 1), ("fb", 0, 0, 1), ("z", 1, 1, 2), ("z", 0, 2, 3),
+    ("fb", 0, 1, 1), ("z", 1, 2, 0), ("sib", 6), ("fb", 1, 1, 1), ("fb", 1, 0, 1), ("z", 1, 2, 1),
+    ("z", 0, 2, 2), ("mid", 1, 0), ("loss", 2), ("z", 0, 2, 0), ("g0", 1, 1), ("g0", 1, 0), ("z", 1, 2, 3),
+    ("mid", 0, 0), ("g0", 0, 1), ("z", 1, 2, 2), ("g0", 0, 0), ("z", 0, 2, 1), ("fb", 0, 1, 2),
+    ("fb", 0, 0, 2), ("fb", 1, 1, 2), ("fb", 1, 0, 2), ("fa", 0, 1, 2), ("fa", 0, 0, 2), ("z", 1, 3, 0),
+    ("z", 0, 3, 3), ("z", 1, 3, 1), ("z", 0, 3, 2), ("mid", 1, 1), ("g1", 1, 1), ("g1", 1, 0), ("z", 0, 3, 0),
+    ("z", 1, 3, 3), ("mid", 0, 1), ("loss", 3), ("g1", 0, 0), ("g1", 0, 1), ("z", 0, 3, 1), ("z", 1, 3, 2),
+    ("mid", 0, 2), ("mid", 1, 2), ("gend", 1), ("zend",), ("gend", 0),
+)
+
+
+def mod(value, size):
+    return lax.rem(value + size, size)
+
+
+def as_row(column, eye):
+    return jnp.sum(jnp.where(eye, column, 0.0), axis=0, keepdims=True)
+
+
+def as_column(row, eye):
+    return jnp.sum(jnp.where(eye, row, 0.0), axis=1, keepdims=True)
+
+
+def kernel(
+    dense,
+    buyers_ref, sellers_ref, elig_ref, pos_ref,
+    bgrad_ref, sgrad_ref, loss_ref,
+    b_all, s_all, bt_all, score, pbuf, qbuf,
+    pos_f, pos_cols, row_stat, col_stat, row_x, row_in, col_x, col_in,
+    row_lse, col_lse, sum_x, sum_in, rl_cols,
+    sib_s, sib_r, z_s, z_r, f0_s, f0_r, f1_s, f1_r, mid, g0_s, g0_r, g1_s, g1_r, seller_t,
+    next_ref, slot_ref, list_ref,
+    send_sem, recv_sem,
+):
+    slots = NZ * NY if dense else score.shape[0]
+    market = lax.axis_index("market")
+    sub = lax.axis_index("sub")
+    z, y = lax.div(market, NY), lax.rem(market, NY)
+    x, c = lax.div(sub, NC), lax.rem(sub, NC)
+    other = 1 - c
+
+    def dev(zz, yy, xx, cc):
+        return (zz * NY + yy, xx * NC + cc)
+
+    def zdev(step):
+        return dev(mod(z + step, NZ), y, x, c)
+
+    def ydev(step):
+        return dev(z, mod(y + step, NY), x, c)
+
+    def xdev(step):
+        return dev(z, y, mod(x + step, NX), c)
+
+    sibling = dev(z, y, x, other)
+
+    row_peers = (
+        sibling,
+        dev(z + 1 - 2 * lax.rem(z, 2), y, x, c),
+        dev(z + 2 - 4 * lax.rem(lax.div(z, 2), 2), y, x, c),
+        dev(mod(z + 4, NZ), y, x, c),
+    )
+    col_peers = (
+        dev(z, y, x + 1 - 2 * lax.rem(x, 2), c),
+        dev(z, y, mod(x + 2, NX), c),
+        dev(z, y + 1 - 2 * lax.rem(y, 2), x, c),
+        dev(z, mod(y + 2, NY), x, c),
+    )
+
+    barrier = pltpu.get_barrier_semaphore()
+    row_steps = [(dz, dc) for dz in (4, 3, 5, 2, 6, 1, 7, 0) for dc in (0, 1) if dz or dc]
+    col_steps = [(dy, dx) for dy in (2, 1, 3, 0) for dx in (2, 1, 3, 0) if dy or dx]
+
+    def core_of(dc):
+        return other if dc else c
+
+    for (dz, dc), (dy, dx) in zip(row_steps, col_steps):
+        for peer in (
+            dev(mod(z + dz, NZ), y, x, core_of(dc)),
+            dev(z, mod(y + dy, NY), mod(x + dx, NX), c),
+        ):
+            pl.semaphore_signal(barrier, inc=1, device_id=peer, device_id_type=MESH)
+    b_all[z, c] = buyers_ref[...].astype(BF16)
+    s_all[y, x] = sellers_ref[...].astype(BF16)
+    own_pos = pos_ref[...] - market * (ROWS * NX * NC)
+    pos_f[c] = jnp.broadcast_to(own_pos.astype(F32), (8, ROWS))
+    pl.semaphore_wait(barrier, 30)
+
+    names = {}
+    landed = set()
+    pending = []
+
+    def sem_of(name):
+        return names.setdefault(name, len(names))
+
+    def send(name, src, dst, device):
+        place = sem_of(name)
+        copy = pltpu.make_async_remote_copy(
+            src_ref=src, dst_ref=dst, send_sem=send_sem.at[place], recv_sem=recv_sem.at[place],
+            device_id=device, device_id_type=MESH,
+        )
+        copy.start()
+        pending.append(copy)
+
+    def arrive(name, dst):
+        place = sem_of(name)
+        pltpu.make_async_remote_copy(
+            src_ref=dst, dst_ref=dst, send_sem=send_sem.at[place], recv_sem=recv_sem.at[place],
+            device_id=sibling, device_id_type=MESH,
+        ).wait_recv()
+
+    def need(name, dst):
+        if name not in landed:
+            landed.add(name)
+            arrive(name, dst)
+
+    def b_at(step, core, lo=0, rows=ROWS):
+        return b_all.at[mod(z + step, NZ), core, pl.ds(lo, rows)]
+
+    def s_at(first_axis, first_step, second_step, lo, rows):
+        if first_axis == "x":
+            return s_all.at[mod(y + second_step, NY), mod(x + first_step, NX), pl.ds(lo, rows)]
+        return s_all.at[mod(y + first_step, NY), mod(x + second_step, NX), pl.ds(lo, rows)]
+
+    halves = (("x", xdev, ydev, 0), ("y", ydev, xdev, 64))
+
+    z_parts = {1: ((0, 32), (32, 32), (64, 64)), -1: ((96, 32), (64, 32), (0, 64))}
+
+    def z_ref(hop, sign, i):
+        lo, rows = z_parts[sign][i]
+        return b_at(-hop * sign, c, lo, rows)
+
+    def have(step):
+        if abs(step) == 4:
+            wanted = [(4, sign, i) for sign in (1, -1) for i in range(2)]
+        else:
+            wanted = [(abs(step), -1 if step > 0 else 1, i) for i in range(3)] if step else []
+        for hop, sign, i in wanted:
+            need(("b", hop, sign, i), z_ref(hop, sign, i))
+
+    def s_ref(kind, h, step1, sign):
+        axis, dev1, dev2, lo = halves[h]
+        part = lo if sign == 1 else lo + 32
+        if kind == "s0":
+            return s_at(axis, -sign, 0, lo, 64)
+        if kind == "s1":
+            return s_at(axis, 2, 0, part, 32)
+        if kind == "s2":
+            return s_at(axis, step1, -sign, lo, 64)
+        return s_at(axis, step1, 2, part, 32)
+
+    def gather_step(kind, *key):
+        if kind == "b":
+            hop, sign, i = key
+            ref = z_ref(hop, sign, i)
+            if hop:
+                need(("b", hop, sign, i), ref)
+            send(("b", hop + 1, sign, i), ref, ref, zdev(sign))
+        elif kind == "bs":
+            step = key[0]
+            have(step)
+            send(("bs", step), b_at(step, c), b_at(step, c), sibling)
+        elif kind == "s0" or kind == "s1":
+            h, sign = key
+            axis, dev1, dev2, lo = halves[h]
+            if kind == "s0":
+                ref = s_at(axis, 0, 0, lo, 64)
+            else:
+                need(("s0", h, sign), s_ref("s0", h, 0, sign))
+                ref = s_at(axis, -sign, 0, lo if sign == 1 else lo + 32, 32)
+            send((kind, h, sign), ref, ref, dev1(sign))
+        else:
+            h, step1, sign = key
+            axis, dev1, dev2, lo = halves[h]
+            if kind == "s2":
+                if abs(step1) == 1:
+                    need(("s0", h, -step1), s_ref("s0", h, 0, -step1))
+                elif step1 == 2:
+                    for way in (1, -1):
+                        need(("s1", h, way), s_ref("s1", h, 0, way))
+                ref = s_at(axis, step1, 0, lo, 64)
+            elif kind == "s3":
+                need(("s2", h, step1, sign), s_ref("s2", h, step1, sign))
+                ref = s_at(axis, step1, -sign, lo if sign == 1 else lo + 32, 32)
+            else:
+                need(("s3", h, step1, sign), s_ref("s3", h, step1, sign))
+                return
+            send((kind, h, step1, sign), ref, ref, dev2(sign))
+
+    early = 8
+    for task in GATHER_ORDER[:early]:
+        gather_step(*task)
+    send(("pos",), pos_f.at[c], pos_f.at[c], sibling)
+
+    own_block = z * NY + y
+
+    def eligible(block):
+        return elig_ref[lax.div(block, NY) * NY + y, z * NY + lax.rem(block, NY)] > 0
+
+    if not dense:
+
+        def walk_back(i, following):
+            block = NZ * NY - 1 - i
+            next_ref[block] = following
+            live = jnp.logical_and(eligible(block), block != own_block)
+            return jnp.where(live, block, following)
+
+        first = lax.fori_loop(0, NZ * NY, walk_back, own_block)
+
+        def rank(block, seen):
+            live = jnp.logical_and(eligible(block), block != own_block)
+            slot_ref[block] = jnp.where(block == own_block, 0, jnp.where(live, 1 + seen, slots))
+            return seen + jnp.where(live, 1, 0)
+
+        lax.fori_loop(0, NZ * NY, rank, 0)
+        list_ref[0] = own_block
+
+        def walk(t, block):
+            list_ref[t] = block
+            return next_ref[block]
+
+        lax.fori_loop(1, slots, walk, first)
+
+    for task in GATHER_ORDER[early:]:
+        gather_step(*task)
+    arrive(("pos",), pos_f.at[other])
+    for step in (0, 1, -1, 2, -2, 3, -3, 4):
+        need(("bs", step), b_at(step, other))
+
+    def flip(zz, carry):
+        for core in range(NC):
+            bt_all[zz, core] = b_all[zz, core].T
+        return carry
+
+    lax.fori_loop(0, NZ, flip, 0)
+
+    eye = lax.broadcasted_iota(jnp.int32, (ROWS, ROWS), 0) == lax.broadcasted_iota(
+        jnp.int32, (ROWS, ROWS), 1
+    )
+    unit = LOG2E / math.sqrt(EMBED)
+
+    for core in range(NC):
+        pos_cols[core * ROWS : (core + 1) * ROWS, :] = jnp.broadcast_to(
+            as_column(pos_f[core, 0:1, :], eye), (ROWS, ROWS)
+        )
+
+    def hits(xx):
+        lane = lax.broadcasted_iota(jnp.int32, (NC * ROWS, ROWS), 1) + (xx * NC + c) * ROWS
+        return pos_cols[...] == lane.astype(F32)
+
+    if not dense:
+        row_stat[slots] = jnp.zeros((8, ROWS), F32)
+        row_stat[slots, 0:2, :] = jnp.full((2, ROWS), neg_fill, F32)
+        col_stat[slots] = jnp.zeros((8, ROWS), F32)
+        col_stat[slots, 0:4, :] = jnp.full((4, ROWS), neg_fill, F32)
+
+    def block_of(t):
+        return t if dense else list_ref[t]
+
+    def slot_of(zz, yy):
+        return zz * NY + yy if dense else slot_ref[zz * NY + yy]
+
+    def first_pass(t, carry):
+        block = block_of(t)
+        left = b_all[lax.div(block, NY)].reshape(NC * ROWS, EMBED)
+        right = s_all[lax.rem(block, NY)].reshape(NX * ROWS, EMBED)
+        tile = (
+            lax.dot_general(left, right, (((1,), (1,)), ((), ())), preferred_element_type=F32)
+            * unit
+        )
+        if dense:
+            tile = jnp.where(eligible(block), tile, neg_fill)
+        score[t] = tile
+        row_top = jnp.max(tile, axis=1, keepdims=True)
+        row_sum = jnp.sum(jnp.exp2(tile - row_top), axis=1, keepdims=True)
+        col_top = jnp.max(tile, axis=0, keepdims=True)
+        col_sum = jnp.sum(jnp.exp2(tile - col_top), axis=0, keepdims=True)
+        for core in range(NC):
+            span = slice(core * ROWS, (core + 1) * ROWS)
+            row_stat[t, core : core + 1, :] = as_row(row_top[span], eye)
+            row_stat[t, 2 + core : 3 + core, :] = as_row(row_sum[span], eye)
+        for xx in range(NX):
+            span = slice(xx * ROWS, (xx + 1) * ROWS)
+            col_stat[t, xx : xx + 1, :] = col_top[:, span]
+            col_stat[t, 4 + xx : 5 + xx, :] = col_sum[:, span]
+        return carry
+
+    def first_pair(i, carry):
+        first_pass(2 * i, 0)
+        first_pass(2 * i + 1, 0)
+        return carry
+
+    lax.fori_loop(0, slots // 2, first_pair, 0)
+    own_slot = own_block if dense else 0
+    matched = jnp.zeros((NC * ROWS, 1), F32)
+    for xx in range(NX):
+        matched = matched + jnp.sum(
+            jnp.where(hits(xx), score[own_slot, :, xx * ROWS : (xx + 1) * ROWS], 0.0),
+            axis=1, keepdims=True,
+        )
+
+    def merge(tops, sums):
+        top = tops[0]
+        for item in tops[1:]:
+            top = jnp.maximum(top, item)
+        total = jnp.zeros_like(top)
+        for item, amount in zip(tops, sums):
+            total = total + amount * jnp.exp2(item - top)
+        return top, total
+
+    for zz in range(NZ):
+        stats = [row_stat[slot_of(zz, yy)] for yy in range(NY)]
+        top, total = merge([a[0:2] for a in stats], [a[2:4] for a in stats])
+        row_x[NC * zz : NC * zz + NC, :] = top + jnp.log2(total)
+    for yy in range(NY):
+        stats = [col_stat[slot_of(zz, yy)] for zz in range(NZ)]
+        top, total = merge([a[0:4] for a in stats], [a[4:8] for a in stats])
+        col_x[NX * yy : NX * yy + NX, :] = top + jnp.log2(total)
+    row_x[16:24, :] = jnp.broadcast_to(jnp.sum(matched, axis=0, keepdims=True), (8, ROWS))
+
+    for (dz, dc), (dy, dx) in zip(row_steps, col_steps):
+        to = dev(mod(z + dz, NZ), y, x, core_of(dc))
+        send(("row", dz, dc), row_x, row_in.at[z * NC + c], to)
+        to = dev(z, mod(y + dy, NY), mod(x + dx, NX), c)
+        send(("col", dy, dx), col_x, col_in.at[y * NX + x], to)
+    row_in[z * NC + c] = row_x[...]
+    col_in[y * NX + x] = col_x[...]
+    for (dz, dc), (dy, dx) in reversed(list(zip(row_steps, col_steps))):
+        arrive(("row", dz, dc), row_in.at[mod(z - dz, NZ) * NC + core_of(dc)])
+        arrive(("col", dy, dx), col_in.at[mod(y - dy, NY) * NX + mod(x - dx, NX)])
+
+    def log_sum(parts):
+        top, total = merge(parts, [1.0] * len(parts))
+        return top + jnp.log2(total)
+
+    row_part = log_sum([row_in[i, 0:16, :] for i in range(16)])
+    col_part = log_sum([col_in[i] for i in range(16)])
+    matched_sum = row_in[0, 16:24, :]
+    for i in range(1, 16):
+        matched_sum = matched_sum + row_in[i, 16:24, :]
+    row_lse[...] = row_part
+    col_lse[...] = col_part
+    line_terms = jnp.sum(jnp.sum(row_part, axis=1, keepdims=True), axis=0, keepdims=True)
+    plane_terms = jnp.sum(jnp.sum(col_part, axis=1, keepdims=True), axis=0, keepdims=True)
+    sum_x[0, 0] = jnp.broadcast_to(line_terms, (8, ROWS)) - 2.0 * matched_sum
+    sum_x[0, 1] = jnp.broadcast_to(plane_terms, (8, ROWS))
+
+    def loss_send(hop):
+        send(("l0", hop), sum_x.at[hop, 0], sum_in.at[hop, 0], col_peers[hop])
+        send(("l1", hop), sum_x.at[hop, 1], sum_in.at[hop, 1], row_peers[hop])
+
+    def loss_add(hop):
+        arrive(("l0", hop), sum_in.at[hop, 0])
+        arrive(("l1", hop), sum_in.at[hop, 1])
+        sum_x[hop + 1] = sum_x[hop] + sum_in[hop]
+
+    for zz in range(NZ):
+        for core in range(NC):
+            place = zz * NC + core
+            rl_cols[zz, core * ROWS : (core + 1) * ROWS, :] = jnp.broadcast_to(
+                as_column(row_lse[place : place + 1, :], eye) + 1.0, (ROWS, ROWS)
+            )
+
+    def second_pass(t, own):
+        block = block_of(t)
+        zz, yy = lax.div(block, NY), lax.rem(block, NY)
+        row_part = rl_cols[zz]
+        parts = []
+        for xx in range(NX):
+            tile = score[t, :, xx * ROWS : (xx + 1) * ROWS]
+            col_part = col_lse[pl.ds(yy * NX + xx, 1), :] + 1.0
+            mixed = jnp.exp2(tile - row_part) + jnp.exp2(tile - col_part)
+            if dense:
+                mixed = mixed - jnp.where(block == own_block, jnp.where(hits(xx), 1.0, 0.0), 0.0)
+            elif own:
+                mixed = mixed - jnp.where(hits(xx), 1.0, 0.0)
+            parts.append(mixed.astype(BF16))
+        weights = jnp.concatenate(parts, axis=1)
+        right = s_all[yy].reshape(NX * ROWS, EMBED)
+        term = jnp.dot(weights, right, preferred_element_type=F32)
+        for core in range(NC):
+            part = term[core * ROWS : (core + 1) * ROWS]
+            if dense:
+                pbuf[zz, core] = pbuf[zz, core] + part
+            else:
+                pbuf[t, core] = part
+        flipped = jnp.concatenate([bt_all[zz, 0], bt_all[zz, 1]], axis=1)
+        term = jnp.dot(flipped, weights, preferred_element_type=F32)
+        for xx in range(NX):
+            part = term[:, xx * ROWS : (xx + 1) * ROWS]
+            if dense:
+                qbuf[yy, xx] = qbuf[yy, xx] + part
+            else:
+                qbuf[t, xx] = part
+
+    def other_blocks(i, carry):
+        second_pass(2 * i, False)
+        second_pass(2 * i + 1, False)
+        return carry
+
+    loss_send(0)
+    if dense:
+        pbuf[...] = jnp.zeros(pbuf.shape, F32)
+        qbuf[...] = jnp.zeros(qbuf.shape, F32)
+        lax.fori_loop(0, slots // 2, other_blocks, 0)
+    else:
+        second_pass(0, True)
+        second_pass(1, False)
+        lax.fori_loop(1, slots // 2, other_blocks, 0)
+        pbuf[slots] = jnp.zeros(pbuf.shape[1:], F32)
+        qbuf[slots] = jnp.zeros(qbuf.shape[1:], F32)
+    step_rows = 32
+
+    def by_rows(lo, rows, body):
+        def at(i, carry):
+            body(pl.multiple_of(lo + i * step_rows, step_rows))
+            return carry
+
+        lax.fori_loop(0, rows // step_rows, at, 0)
+
+    def p_sum(zz, core, at):
+        if dense:
+            return pbuf[zz, core, pl.ds(at, step_rows), :]
+        total = None
+        for yy in range(NY):
+            term = pbuf[slot_of(zz, yy), core, pl.ds(at, step_rows), :]
+            total = term if total is None else total + term
+        return total
+
+    def q_sum(yy, xx, at):
+        if dense:
+            return qbuf[yy, xx, pl.ds(at, step_rows), :]
+        total = None
+        for zz in range(NZ):
+            term = qbuf[slot_of(zz, yy), xx, pl.ds(at, step_rows), :]
+            total = term if total is None else total + term
+        return total
+
+    def to_f32(ref, place, at):
+        return ref[(*place, pl.ds(at, step_rows))].astype(F32)
+
+    order = (4, 3, -3, 2, -2, 1, -1, 0)
+
+    def sib_send(place):
+        def fill(at):
+            value = p_sum(mod(z + order[place], NZ), other, at)
+            sib_s[place, pl.ds(at, step_rows), :] = value.astype(BF16)
+
+        by_rows(0, ROWS, fill)
+        send(("gs", place), sib_s.at[place], sib_r.at[place], sibling)
+
+    def z_value(place, at):
+        return p_sum(mod(z + order[place], NZ), c, at) + to_f32(sib_r, (place,), at)
+
+    z_places = ((0, 1, 3, 5), (0, 2, 4, 6))
+
+    def z_send(d, hop, i):
+        sign, lo, place = 1 - 2 * d, 32 * i, z_places[d][hop]
+        started = hop == 0 or (hop == 1 and (lo < 64) == (d == 1))
+        need(("gs", place), sib_r.at[place])
+        if not started:
+            arrive(("gz", d, hop - 1, i), z_r.at[d, hop - 1, pl.ds(lo, 32)])
+        value = z_value(place, lo)
+        if not started:
+            value = value + to_f32(z_r, (d, hop - 1,), lo)
+        z_s[d, hop, pl.ds(lo, 32), :] = value.astype(BF16)
+        part = pl.ds(lo, 32)
+        send(("gz", d, hop, i), z_s.at[d, hop, part], z_r.at[d, hop, part], zdev(sign))
+
+    grads = (("y", ydev, xdev, 0, x), ("x", xdev, ydev, 256, y))
+    offsets = (2, 1, -1, 0)
+    groups = ((0,), (1, 2), (3,))
+
+    def q_at(axis, step, lane, at):
+        if axis == "y":
+            return q_sum(mod(y + step, NY), lane, at)
+        return q_sum(lane, mod(x + step, NX), at)
+
+    def f_send(kind, h, d, g):
+        axis, dev1, dev2, base, place = grads[h]
+        sign = 1 - 2 * d
+        group = groups[g]
+        part = pl.ds(group[0], len(group))
+        half = 1 - d if kind == "fa" else d
+        if kind == "fb":
+            arrive(("f0", h, d, g), f0_r.at[h, d, part])
+        for k in group:
+            def fill(at):
+                step = 2 if kind == "f0" else sign
+                value = q_at(axis, step, mod(place + offsets[k], 4), base + half * 128 + at)
+                if kind == "f0":
+                    f0_s[h, d, k, pl.ds(at, step_rows), :] = value.astype(BF16)
+                    return
+                if kind == "fb":
+                    value = value + to_f32(f0_r, (h, d, k,), at)
+                f1_s[h, d, half, k, pl.ds(at, step_rows), :] = value.astype(BF16)
+
+            by_rows(0, 128, fill)
+        if kind == "f0":
+            send((kind, h, d, g), f0_s.at[h, d, part], f0_r.at[h, d, part], dev1(sign))
+        else:
+            send((kind, h, d, g), f1_s.at[h, d, half, part], f1_r.at[h, d, half, part], dev1(sign))
+
+    def mid_sum(h, g):
+        axis, dev1, dev2, base, place = grads[h]
+        group = groups[g]
+        part = pl.ds(group[0], len(group))
+        for d in range(2):
+            arrive(("fa", h, d, g), f1_r.at[h, d, 1 - d, part])
+            arrive(("fb", h, d, g), f1_r.at[h, d, d, part])
+        for k in group:
+            for half in range(2):
+                def fill(at):
+                    value = q_at(axis, 0, mod(place + offsets[k], 4), base + half * 128 + at)
+                    value = value + to_f32(f1_r, (h, 0, half, k,), at)
+                    value = value + to_f32(f1_r, (h, 1, half, k,), at)
+                    mid[h, k, pl.ds(half * 128 + at, step_rows), :] = value
+
+                by_rows(0, 128, fill)
+
+    def g_send(kind, h, d):
+        axis, dev1, dev2, base, place = grads[h]
+        sign = 1 - 2 * d
+        far_lo, near_lo = d * 128, 128 - d * 128
+        if kind == "g0":
+            g0_s[h, d] = mid[h, 0, far_lo : far_lo + 128, :].astype(BF16)
+            send(("g0", h, d), g0_s.at[h, d], g0_r.at[h, d], dev2(sign))
+            return
+        arrive(("g0", h, d), g0_r.at[h, d])
+        g1_s[h, d, near_lo : near_lo + 128, :] = mid[h, 1 + d, near_lo : near_lo + 128, :].astype(BF16)
+        g1_s[h, d, far_lo : far_lo + 128, :] = (
+            mid[h, 1 + d, far_lo : far_lo + 128, :] + g0_r[h, d].astype(F32)
+        ).astype(BF16)
+        send(("g1", h, d), g1_s.at[h, d], g1_r.at[h, d], dev2(sign))
+
+    def g_end(h):
+        for d in range(2):
+            arrive(("g1", h, d), g1_r.at[h, d])
+        seller_t[h * 256 : (h + 1) * 256, :] = (
+            mid[h, 3] + g1_r[h, 0].astype(F32) + g1_r[h, 1].astype(F32)
+        )
+
+    def z_end():
+        need(("gs", 7), sib_r.at[7])
+        for d in range(2):
+            for i in range(4):
+                arrive(("gz", d, 3, i), z_r.at[d, 3, pl.ds(32 * i, 32)])
+
+        def finish(at):
+            bgrad_ref[pl.ds(at, step_rows), :] = (
+                z_value(7, at) + to_f32(z_r, (0, 3,), at) + to_f32(z_r, (1, 3,), at)
+            )
+
+        by_rows(0, ROWS, finish)
+
+    def loss_step(hop):
+        loss_add(hop)
+        if hop < 3:
+            loss_send(hop + 1)
+
+    actions = {
+        "sib": sib_send, "z": z_send, "zend": z_end, "mid": mid_sum, "gend": g_end, "loss": loss_step,
+    }
+    for task in RETURN_ORDER:
+        if task[0] in actions:
+            actions[task[0]](*task[1:])
+        elif task[0] in ("g0", "g1"):
+            g_send(*task)
+        else:
+            f_send(*task)
+    sgrad_ref[...] = seller_t[...].T
+    loss_ref[...] = (sum_x[4, 0, 0:1, :] + sum_x[4, 1, 0:1, :]) * (
+        math.log(2.0) / (2.0 * ROWS * NZ * NY * NX * NC)
+    )
+    for copy in pending:
+        copy.wait_send()
+
+
+def vmem(shape, dtype):
+    return pltpu.VMEM(shape, dtype)
+
+
+def fused(dense, slots, buyers, sellers, eligibility, positives):
+    extra = 0 if dense else 1
+    scratch = [
+        vmem((NZ, NC, ROWS, EMBED), BF16),
+        vmem((NY, NX, ROWS, EMBED), BF16),
+        vmem((NZ, NC, EMBED, ROWS), BF16),
+        vmem((slots, NC * ROWS, NX * ROWS), F32),
+        vmem((NZ if dense else slots + 1, NC, ROWS, EMBED), F32),
+        vmem((NY if dense else slots + 1, NX, EMBED, ROWS), F32),
+        vmem((NC, 8, ROWS), F32),
+        vmem((NC * ROWS, ROWS), F32),
+        vmem((slots + extra, 8, ROWS), F32),
+        vmem((slots + extra, 8, ROWS), F32),
+        vmem((24, ROWS), F32),
+        vmem((16, 24, ROWS), F32),
+        vmem((16, ROWS), F32),
+        vmem((16, 16, ROWS), F32),
+        vmem((16, ROWS), F32),
+        vmem((16, ROWS), F32),
+        vmem((5, 2, 8, ROWS), F32),
+        vmem((4, 2, 8, ROWS), F32),
+        vmem((NZ, NC * ROWS, ROWS), F32),
+        vmem((NZ, ROWS, EMBED), BF16),
+        vmem((NZ, ROWS, EMBED), BF16),
+        vmem((2, 4, ROWS, EMBED), BF16),
+        vmem((2, 4, ROWS, EMBED), BF16),
+        vmem((2, 2, 4, 128, ROWS), BF16),
+        vmem((2, 2, 4, 128, ROWS), BF16),
+        vmem((2, 2, 2, 4, 128, ROWS), BF16),
+        vmem((2, 2, 2, 4, 128, ROWS), BF16),
+        vmem((2, 4, 256, ROWS), F32),
+        vmem((2, 2, 128, ROWS), BF16),
+        vmem((2, 2, 128, ROWS), BF16),
+        vmem((2, 2, 256, ROWS), BF16),
+        vmem((2, 2, 256, ROWS), BF16),
+        vmem((EMBED, ROWS), F32),
+        pltpu.SMEM((NZ * NY,), jnp.int32),
+        pltpu.SMEM((NZ * NY,), jnp.int32),
+        pltpu.SMEM((slots,), jnp.int32),
+        pltpu.SemaphoreType.DMA((224,)),
+        pltpu.SemaphoreType.DMA((224,)),
+    ]
+    in_vmem = pl.BlockSpec(memory_space=pltpu.VMEM)
+    buyer_grad, seller_grad, loss = pl.pallas_call(
+        functools.partial(kernel, dense),
+        out_shape=(
+            jax.ShapeDtypeStruct((ROWS, EMBED), F32),
+            jax.ShapeDtypeStruct((ROWS, EMBED), F32),
+            jax.ShapeDtypeStruct((1, ROWS), F32),
+        ),
+        in_specs=[in_vmem, in_vmem, pl.BlockSpec(memory_space=pltpu.SMEM), in_vmem],
+        out_specs=(in_vmem, in_vmem, in_vmem),
+        scratch_shapes=scratch,
+        compiler_params=pltpu.CompilerParams(
+            collective_id=1 if dense else 0, has_side_effects=True, vmem_limit_bytes=60 * 1024 * 1024
+        ),
+        name="two_tower_dense" if dense else "two_tower",
+    )(buyers, sellers, eligibility, positives.reshape(1, ROWS))
+    return (buyer_grad, seller_grad, loss[0, 0])
+
+
+def ring_step(value, axis):
+    count = lax.axis_size(axis)
+    return lax.ppermute(value, axis, [(i, (i + 1) % count) for i in range(count)])
+
+
+def ring_gather(value, axis):
+    count, me = lax.axis_size(axis), lax.axis_index(axis)
+    start = jnp.zeros((count, *value.shape), value.dtype)
+    start = lax.dynamic_update_index_in_dim(start, value, me, 0)
+
+    def step(k, state):
+        block, whole = state
+        block = ring_step(block, axis)
+        place = lax.rem(me - k + count, count)
+        return (block, lax.dynamic_update_index_in_dim(whole, block, place, 0))
+
+    return lax.fori_loop(1, count, step, (value, start))[1]
+
+
+def ring_scatter(whole, axis):
+    count, me = lax.axis_size(axis), lax.axis_index(axis)
+    parts = whole.reshape(count, -1, whole.shape[-1])
+
+    def take(place):
+        return lax.dynamic_index_in_dim(parts, lax.rem(place + 2 * count, count), 0, False)
+
+    def step(k, total):
+        return ring_step(total, axis) + take(me - 1 - k)
+
+    return lax.fori_loop(1, count, step, take(me - 1))
 
 
 def merged(part, axis, combine):
-    gathered = jax.tree.map(lambda a: lax.all_gather(a, axis), part)
+    gathered = jax.tree.map(lambda a: ring_gather(a, axis), part)
 
     def take(source):
         return jax.tree.map(lambda a: lax.dynamic_index_in_dim(a, source, 0, False), gathered)
@@ -63,7 +773,7 @@
     return lax.scan(outer, totals, jnp.arange(group_count // 4))
 
 
-def shards(buyers, sellers, eligibility, positives):
+def general(buyers, sellers, eligibility, positives):
     row_count, embed_width = buyers.shape
     sub_count = lax.axis_size("sub")
     group_count = lax.axis_size("market")
@@ -75,10 +785,10 @@
     buyer_half = buyers.astype(jnp.bfloat16)
     seller_half = sellers.astype(jnp.bfloat16)
     group_buyers, group_pos = (
-        lax.all_gather(buyer_half, "sub", axis=0, tiled=True),
-        lax.all_gather(positives, "sub", axis=0, tiled=True),
-    )
-    seller_panel = lax.all_gather(seller_half, "market", axis=0, tiled=True)
+        ring_gather(buyer_half, "sub").reshape(-1, embed_width),
+        ring_gather(positives, "sub").reshape(-1),
+    )
+    seller_panel = ring_gather(seller_half, "market").reshape(-1, embed_width)
     own_row = lax.dynamic_index_in_dim(eligibility, market_pos, 0, keepdims=False)
 
     def panel_block(target):
@@ -128,7 +838,8 @@
     col_own = lax.dynamic_slice_in_dim(col_lse, market_pos * row_count, row_count, 0)
     pos_own = lax.dynamic_slice_in_dim(pos_logits, sub_pos * row_count, row_count, 0)
     local_loss = jnp.sum(row_own) + jnp.sum(col_own) - 2.0 * jnp.sum(pos_own)
-    total_loss = lax.psum(local_loss, ("market", "sub"))
+    total_loss = jnp.sum(ring_gather(local_loss.reshape(1), "sub"))
+    total_loss = jnp.sum(ring_gather(total_loss.reshape(1), "market"))
     loss = total_loss / (2.0 * group_rows * group_count)
 
     def grad_step(state, target, is_live):
@@ -154,7 +865,7 @@
         own_row,
         group_count,
     )
-    buyer_grad = lax.psum_scatter(acc, "sub", scatter_dimension=0, tiled=True)
+    buyer_grad = ring_scatter(acc, "sub")
     row_span = lax.axis_size("market") * row_count
 
     def one_group(offset):
@@ -183,10 +894,19 @@
         return lax.cond(own_row[offset] > 0, one_live_branch, one_dead_branch, None)
 
     pieces = lax.map(one_group, jnp.arange(row_span // row_count))
-    seller_grad = lax.psum_scatter(
-        pieces.reshape(row_span, embed_width), "market", scatter_dimension=0, tiled=True
-    )
+    seller_grad = ring_scatter(pieces.reshape(row_span, embed_width), "market")
     return (buyer_grad, seller_grad, loss)
+
+
+def shards(buyers, sellers, eligibility, positives):
+    blocks = (eligibility > 0).astype(jnp.int32).reshape(NZ, NY, NZ, NY)
+    busiest = jnp.max(jnp.sum(blocks, axis=(0, 3)))
+    return lax.cond(
+        busiest <= SLOTS,
+        functools.partial(fused, False, SLOTS),
+        general,
+        buyers, sellers, eligibility, positives,
+    )
 
 
 def solution(mesh):

time: 859 us -> 78.6 us (0.09)
  blocking collectives: 296 us -> 0 us
  waiting for transfers between devices: 236 us -> 0 us
  loops' own time: 148 us -> 0.87 us
  local copies, waits for them, and re-layouts: 103 us -> 2.16 us
  Pallas kernels: 0 us -> 71.3 us
  matrix products: 37.2 us -> 0 us
  between operations: 17.6 us -> 2.43 us
  other arithmetic: 16.4 us -> 1.51 us
    all_gather x6 -> x0, blocking collectives: 169 us -> none  [the longest x5 159 us: merged(): gathered = jax.tree.map(lambda a: lax.all_gather(a, axis), part)]
    reduce_scatter x2 -> x0, waiting for transfers between devices: 147 us -> none  [the longest x1 147 us: shards(): lax.psum_scatter(pieces.reshape(row_span, embed_width), 'market', scatter...]
    another operation x101 -> x1, loops' own time: 148 us -> 0.87 us  [shards(): lax.cond(busiest <= SLOTS, functools.partial(fused, False, SLOTS), genera...]
    psum x1 -> x0, blocking collectives: 127 us -> none  [shards(): total_loss = lax.psum(local_loss, ('market', 'sub'))]
    all_gather x2 -> x0, waiting for transfers between devices: 88.9 us -> none  [the longest x1 72.1 us: shards(): seller_panel = lax.all_gather(seller_half, 'market', axis=0, tiled=True)]
    pallas_call x0 -> x1, Pallas kernels: none -> 71.3 us  [fused(): pl.pallas_call(functools.partial(kernel, dense), out_shape=(jax.ShapeDtyp...]
    dynamic_slice x159 -> x0, local copies, waits for them, and re-layouts: 62.2 us -> none  [the longest x32 21.5 us: one_group(): return lax.cond(own_row[offset] > 0, one_live_branch, one_dead_branch, None)]
    dot_general x19 -> x0, matrix products: 37.2 us -> none  [the longest x7 16.3 us: tile_scores(): lax.dot_general(left, right, (((1,), (1,)), ((), ())), preferred_element_...]
  transfers between devices with their start and end apart: 4 -> 0, of which waited for: 3 -> 0; matrix products, arithmetic and copies ran while one was open for 9% -> 0% of each run, Pallas kernels for 0% -> 0%
where the time goes in v2:
time: 78.6 us; the launch traced here: 78.3 us
  Pallas kernels  71.3 us (91%)
  between operations  2.43 us (3%)
  local copies, waits for them, and re-layouts  2.16 us (3%)
  other arithmetic  1.51 us (2%)
  loops' own time  0.87 us (1%)
    pallas_call x1, Pallas kernels, fused(): pl.pallas_call(functools.partial(kernel, dense), out_shape=(jax.ShapeDtyp...  71.3 us
    unnamed x3, local copies, waits for them, and re-layouts  2.06 us

profile of v2, /device:TPU:2, one launch (start us, length us, event | category | flops | bytes accessed | tf_op | source)
XLA Modules:
  0.0 78.3 jit_solution(15527018399030428025)
XLA Ops:
  0.6 0.7 copy.236
  1.3 0.7 compare_convert_fusion
  2.0 0.1 reshape.131
  2.1 0.2 reduce_sum.135
  2.3 0.6 reduce_max.81
  3.6 72.2 %conditional.10 = (f32[128,512]{1,0:T(8,128)S(1)}, f32[128,512]{1,0:T(8,128)S(1)}, f32[]{:T(128)}) conditional(s32[]{:T(128)} %convert_element_type.103, (s32[32,32]{1,0:T(8,128)}, f32[128,512]{1,0:T(8,128)}, f32[128,512]{1,0:T(8,128)}, s32[128]{0:T(128)S(1)}) %tuple.352, (s32[128]{0:T(128)S(1)}, f32[128,512]{1,0:T(8,128)}, f32[128,512]{1,0:T(8,128)}, ...), branch_computations={%region_2.77_spmd, %region_77.78_spmd} | conditional | flops 2025764992 | bytes 71768840 | solution.py:904
  3.8 71.3 %two_tower.1 = (f32[128,512]{1,0:T(8,128)S(1)}, f32[128,512]{1,0:T(8,128)S(1)}, f32[1,128]{1,0:T(1,128)}) custom-call(f32[128,512]{1,0:T(8,128)} %get-tuple-element.1952.buyers_ref, f32[128,512]{1,0:T(8,128)} %get-tuple-element.1953.sellers_ref, s32[32,32]{1,0:T(8,128)} %get-tuple-element.1954.elig_ref, s32[1,128]{1,0:T(1,128)S(1)} %bitcast.230), custom_call_target="tpu_custom_call" | custom-call | tf_op jit(solution)/shard_map/cond/branch_1_fun/two_tower/pallas_call | solution.py:671
  75.8 0.7 copy.237
  76.5 0.7 copy.238

commit v3 on v2

--- a/solution.py
+++ b/solution.py
@@ -21,20 +21,22 @@
 
 GATHER_ORDER = (
     ("b", 0, -1, 0), ("s0", 0, -1), ("bs", 0), ("b", 0, 1, 0), ("s0", 0, 1), ("s0", 1, 1), ("s2", 1, 0, 1),
-    ("s0", 1, -1), ("b", 0, -1, 2), ("b", 0, 1, 1), ("b", 0, -1, 1), ("b", 0, 1, 2), ("s2", 0, 0, -1),
-    ("s2", 0, 0, 1), ("s2", 1, 0, -1), ("b", 1, -1, 0), ("s2", 0, 1, 1), ("b", 1, 1, 0), ("s2", 1, -1, 1),
-    ("s2", 0, 1, -1), ("s1", 0, -1), ("s1", 1, -1), ("b", 1, -1, 1), ("b", 1, 1, 1), ("b", 1, -1, 2),
-    ("s1", 1, 1), ("s1", 0, 1), ("b", 1, 1, 2), ("s3", 0, 0, -1), ("s2", 1, 1, -1), ("s2", 1, 1, 1),
-    ("s2", 1, -1, -1), ("s2", 0, -1, 1), ("s3", 0, 1, 1), ("b", 2, -1, 0), ("b", 2, 1, 1), ("s2", 0, -1, -1),
-    ("b", 2, -1, 1), ("b", 2, 1, 0), ("s2", 1, 2, 1), ("b", 2, -1, 2), ("s2", 1, 2, -1), ("b", 2, 1, 2),
-    ("s2", 0, 2, -1), ("s4", 0, 0, -1), ("bs", 2), ("s2", 0, 2, 1), ("bs", 1), ("bs", -2), ("s3", 1, 0, 1),
-    ("s3", 1, -1, 1), ("s4", 0, 1, 1), ("b", 3, 1, 1), ("b", 3, -1, 0), ("s3", 1, 1, -1), ("b", 3, 1, 0),
-    ("b", 3, -1, 1), ("s3", 0, -1, 1), ("s3", 1, -1, -1), ("s3", 0, 1, -1), ("s3", 1, 0, -1), ("s3", 1, 1, 1),
-    ("bs", -1), ("s3", 0, 0, 1), ("s3", 1, 2, 1), ("s3", 0, -1, -1), ("bs", 3), ("s3", 1, 2, -1),
-    ("s3", 0, 2, -1), ("s3", 0, 2, 1), ("bs", -3), ("bs", 4), ("s4", 1, 0, 1), ("s4", 1, 1, -1),
-    ("s4", 0, -1, 1), ("s4", 1, 0, -1), ("s4", 0, -1, -1), ("s4", 1, -1, -1), ("s4", 1, -1, 1),
-    ("s4", 1, 1, 1), ("s4", 0, 2, 1), ("s4", 0, 1, -1), ("s4", 0, 0, 1), ("s4", 0, 2, -1), ("s4", 1, 2, 1),
-    ("s4", 1, 2, -1),
+    ("s0", 1, -1), ("b", 0, -1, 2), ("b", 0, 1, 1), ("b", 0, -1, 1), ("b", 0, 1, 2), ("flip", 0, 1),
+    ("s2", 0, 0, -1), ("s2", 0, 0, 1), ("s2", 1, 0, -1), ("b", 1, -1, 0), ("s2", 0, 1, 1), ("b", 1, 1, 0),
+    ("s2", 1, -1, 1), ("s2", 0, 1, -1), ("s1", 0, -1), ("s1", 1, -1), ("b", 1, -1, 1), ("b", 1, 1, 1),
+    ("b", 1, -1, 2), ("s1", 1, 1), ("s1", 0, 1), ("b", 1, 1, 2), ("s3", 0, 0, -1), ("s2", 1, 1, -1),
+    ("s2", 1, 1, 1), ("s2", 1, -1, -1), ("s2", 0, -1, 1), ("s3", 0, 1, 1), ("b", 2, -1, 0), ("b", 2, 1, 1),
+    ("s2", 0, -1, -1), ("flip", 0, 0), ("flip", -1, 0), ("b", 2, -1, 1), ("b", 2, 1, 0), ("s2", 1, 2, 1),
+    ("b", 2, -1, 2), ("s2", 1, 2, -1), ("b", 2, 1, 2), ("s2", 0, 2, -1), ("s4", 0, 0, -1), ("bs", 2),
+    ("s2", 0, 2, 1), ("bs", 1), ("bs", -2), ("s3", 1, 0, 1), ("s3", 1, -1, 1), ("s4", 0, 1, 1),
+    ("b", 3, 1, 1), ("b", 3, -1, 0), ("s3", 1, 1, -1), ("flip", -2, 0), ("b", 3, 1, 0), ("b", 3, -1, 1),
+    ("s3", 0, -1, 1), ("s3", 1, -1, -1), ("s3", 0, 1, -1), ("s3", 1, 0, -1), ("s3", 1, 1, 1), ("bs", -1),
+    ("flip", 2, 0), ("s3", 0, 0, 1), ("s3", 1, 2, 1), ("s3", 0, -1, -1), ("flip", -2, 1), ("flip", 2, 1),
+    ("flip", 1, 1), ("bs", 3), ("s3", 1, 2, -1), ("s3", 0, 2, -1), ("s3", 0, 2, 1), ("flip", -3, 0),
+    ("bs", -3), ("bs", 4), ("flip", 3, 0), ("s4", 1, 0, 1), ("flip", 4, 0), ("flip", 3, 1), ("s4", 1, 1, -1),
+    ("flip", -1, 1), ("s4", 0, -1, 1), ("flip", 1, 0), ("s4", 1, 0, -1), ("s4", 0, -1, -1), ("s4", 1, -1, -1),
+    ("s4", 1, -1, 1), ("flip", -3, 1), ("s4", 1, 1, 1), ("s4", 0, 2, 1), ("s4", 0, 1, -1), ("s4", 0, 0, 1),
+    ("s4", 0, 2, -1), ("s4", 1, 2, 1), ("s4", 1, 2, -1), ("flip", 4, 1),
 )
 RETURN_ORDER = (
     ("f0", 1, 1, 0), ("sib", 0), ("f0", 1, 0, 0), ("f0", 0, 0, 0), ("f0", 0, 1, 2), ("sib", 4),
@@ -205,6 +207,13 @@
             step = key[0]
             have(step)
             send(("bs", step), b_at(step, c), b_at(step, c), sibling)
+        elif kind == "flip":
+            step, theirs = key
+            if theirs:
+                need(("bs", step), b_at(step, other))
+            else:
+                have(step)
+            flip(step, other if theirs else c)
         elif kind == "s0" or kind == "s1":
             h, sign = key
             axis, dev1, dev2, lo = halves[h]
@@ -232,6 +241,10 @@
                 return
             send((kind, h, step1, sign), ref, ref, dev2(sign))
 
+    def flip(step, core):
+        zz = mod(z + step, NZ)
+        bt_all[zz, core] = b_all[zz, core].T
+
     early = 8
     for task in GATHER_ORDER[:early]:
         gather_step(*task)
@@ -269,15 +282,6 @@
     for task in GATHER_ORDER[early:]:
         gather_step(*task)
     arrive(("pos",), pos_f.at[other])
-    for step in (0, 1, -1, 2, -2, 3, -3, 4):
-        need(("bs", step), b_at(step, other))
-
-    def flip(zz, carry):
-        for core in range(NC):
-            bt_all[zz, core] = b_all[zz, core].T
-        return carry
-
-    lax.fori_loop(0, NZ, flip, 0)
 
     eye = lax.broadcasted_iota(jnp.int32, (ROWS, ROWS), 0) == lax.broadcasted_iota(
         jnp.int32, (ROWS, ROWS), 1
@@ -686,225 +690,13 @@
     return (buyer_grad, seller_grad, loss[0, 0])
 
 
-def ring_step(value, axis):
-    count = lax.axis_size(axis)
-    return lax.ppermute(value, axis, [(i, (i + 1) % count) for i in range(count)])
-
-
-def ring_gather(value, axis):
-    count, me = lax.axis_size(axis), lax.axis_index(axis)
-    start = jnp.zeros((count, *value.shape), value.dtype)
-    start = lax.dynamic_update_index_in_dim(start, value, me, 0)
-
-    def step(k, state):
-        block, whole = state
-        block = ring_step(block, axis)
-        place = lax.rem(me - k + count, count)
-        return (block, lax.dynamic_update_index_in_dim(whole, block, place, 0))
-
-    return lax.fori_loop(1, count, step, (value, start))[1]
-
-
-def ring_scatter(whole, axis):
-    count, me = lax.axis_size(axis), lax.axis_index(axis)
-    parts = whole.reshape(count, -1, whole.shape[-1])
-
-    def take(place):
-        return lax.dynamic_index_in_dim(parts, lax.rem(place + 2 * count, count), 0, False)
-
-    def step(k, total):
-        return ring_step(total, axis) + take(me - 1 - k)
-
-    return lax.fori_loop(1, count, step, take(me - 1))
-
-
-def merged(part, axis, combine):
-    gathered = jax.tree.map(lambda a: ring_gather(a, axis), part)
-
-    def take(source):
-        return jax.tree.map(lambda a: lax.dynamic_index_in_dim(a, source, 0, False), gathered)
-
-    return lax.fori_loop(
-        1, lax.axis_size(axis), lambda source, state: combine(state, take(source)), take(0)
-    )
-
-
-def tile_scores(left, right, factor):
-    return (
-        lax.dot_general(left, right, (((1,), (1,)), ((), ())), preferred_element_type=jnp.float32)
-        * factor
-    )
-
-
-def row_combine(first_part, second_part):
-    top = jnp.maximum(first_part[0], second_part[0])
-    total = first_part[1] * jnp.exp(first_part[0] - top) + second_part[1] * jnp.exp(
-        second_part[0] - top
-    )
-    return (top, total, first_part[2] + second_part[2])
-
-
-def col_combine(first_part, second_part):
-    top = jnp.maximum(first_part[0], second_part[0])
-    total = first_part[1] * jnp.exp(first_part[0] - top) + second_part[1] * jnp.exp(
-        second_part[0] - top
-    )
-    return (top, total)
-
-
-def coefficient(scores, row_lse, col_lse, is_hit):
-    mixed = 0.5 * (jnp.exp(scores - row_lse) + jnp.exp(scores - col_lse)) - jnp.where(
-        is_hit, 1.0, 0.0
-    )
-    return mixed.astype(jnp.bfloat16)
-
-
-def sweep_groups(stats_step, totals, flags, group_count):
-
-    def outer(state, block_idx):
-        outputs = []
-        for offset in range(4):
-            target = block_idx * 4 + offset
-            state, result = stats_step(state, target, flags[target] > 0)
-            outputs.append(result)
-        stacked = jax.tree.map(lambda *items: jnp.stack(items), *outputs)
-        return (state, stacked)
-
-    return lax.scan(outer, totals, jnp.arange(group_count // 4))
-
-
-def general(buyers, sellers, eligibility, positives):
-    row_count, embed_width = buyers.shape
-    sub_count = lax.axis_size("sub")
-    group_count = lax.axis_size("market")
-    group_rows = row_count * sub_count
-    market_pos = lax.axis_index("market")
-    sub_pos = lax.axis_index("sub")
-    factor = 1.0 / math.sqrt(embed_width)
-    local_cols = jnp.arange(row_count, dtype=jnp.int32)
-    buyer_half = buyers.astype(jnp.bfloat16)
-    seller_half = sellers.astype(jnp.bfloat16)
-    group_buyers, group_pos = (
-        ring_gather(buyer_half, "sub").reshape(-1, embed_width),
-        ring_gather(positives, "sub").reshape(-1),
-    )
-    seller_panel = ring_gather(seller_half, "market").reshape(-1, embed_width)
-    own_row = lax.dynamic_index_in_dim(eligibility, market_pos, 0, keepdims=False)
-
-    def panel_block(target):
-        return lax.dynamic_slice_in_dim(seller_panel, target * row_count, row_count, 0)
-
-    def stats_step(state, target, is_live):
-        row_max, row_sum = state
-
-        def stats_live_branch(unused):
-            scores = tile_scores(group_buyers, panel_block(target), factor)
-            new_max = jnp.maximum(row_max, jnp.max(scores, axis=1))
-            new_sum = row_sum * jnp.exp(row_max - new_max) + jnp.sum(
-                jnp.exp(scores - new_max[:, None]), axis=1
-            )
-            col_top = jnp.max(scores, axis=0)
-            col_total = jnp.sum(jnp.exp(scores - col_top[None, :]), axis=0)
-            return ((new_max, new_sum), (col_top, col_total))
-
-        def stats_dead_branch(unused):
-            return (
-                (row_max, row_sum),
-                (
-                    jnp.full((row_count,), neg_fill, jnp.float32),
-                    jnp.zeros((row_count,), jnp.float32),
-                ),
-            )
-
-        return lax.cond(is_live, stats_live_branch, stats_dead_branch, None)
-
-    start_state = (
-        jnp.full((group_rows,), neg_fill, jnp.float32),
-        jnp.zeros((group_rows,), jnp.float32),
-    )
-    (row_max, row_sum), (col_top, col_total) = sweep_groups(
-        stats_step, start_state, own_row, group_count
-    )
-    col_top = col_top.reshape(group_count * row_count)
-    col_total = col_total.reshape(group_count * row_count)
-    own_scores = tile_scores(group_buyers, seller_half, factor)
-    own_ids = (market_pos * sub_count + sub_pos) * row_count + local_cols
-    pos_part = jnp.sum(jnp.where(group_pos[:, None] == own_ids[None, :], own_scores, 0.0), axis=1)
-    row_max, row_sum, pos_logits = merged((row_max, row_sum, pos_part), "sub", row_combine)
-    col_top, col_total = merged((col_top, col_total), "market", col_combine)
-    row_lse = row_max + jnp.log(row_sum)
-    col_lse = col_top + jnp.log(col_total)
-    row_own = lax.dynamic_slice_in_dim(row_lse, sub_pos * row_count, row_count, 0)
-    col_own = lax.dynamic_slice_in_dim(col_lse, market_pos * row_count, row_count, 0)
-    pos_own = lax.dynamic_slice_in_dim(pos_logits, sub_pos * row_count, row_count, 0)
-    local_loss = jnp.sum(row_own) + jnp.sum(col_own) - 2.0 * jnp.sum(pos_own)
-    total_loss = jnp.sum(ring_gather(local_loss.reshape(1), "sub"))
-    total_loss = jnp.sum(ring_gather(total_loss.reshape(1), "market"))
-    loss = total_loss / (2.0 * group_rows * group_count)
-
-    def grad_step(state, target, is_live):
-
-        def grad_live_branch(acc):
-            block = panel_block(target)
-            scores = tile_scores(group_buyers, block, factor)
-            block_lse = lax.dynamic_slice_in_dim(col_lse, target * row_count, row_count, 0)
-            block_ids = (target * sub_count + sub_pos) * row_count + local_cols
-            weights_half = coefficient(
-                scores,
-                row_lse[:, None],
-                block_lse[None, :],
-                group_pos[:, None] == block_ids[None, :],
-            )
-            return acc + jnp.dot(weights_half, block, preferred_element_type=jnp.float32)
-
-        return (lax.cond(is_live, grad_live_branch, lambda acc: acc, state), None)
-
-    acc, unused = sweep_groups(
-        grad_step,
-        jnp.zeros((lax.axis_size("sub") * row_count, embed_width), jnp.float32),
-        own_row,
-        group_count,
-    )
-    buyer_grad = ring_scatter(acc, "sub")
-    row_span = lax.axis_size("market") * row_count
-
-    def one_group(offset):
-
-        def one_live_branch(unused):
-            block = panel_block(offset)
-            scores = tile_scores(group_buyers, block, factor)
-            block_lse = lax.dynamic_slice_in_dim(col_lse, offset * row_count, row_count, 0)
-            block_ids = (offset * sub_count + sub_pos) * row_count + local_cols
-            weights_half = coefficient(
-                scores,
-                row_lse[:, None],
-                block_lse[None, :],
-                group_pos[:, None] == block_ids[None, :],
-            )
-            return lax.dot_general(
-                weights_half,
-                group_buyers,
-                (((0,), (0,)), ((), ())),
-                preferred_element_type=jnp.float32,
-            )
-
-        def one_dead_branch(unused):
-            return jnp.zeros((row_count, embed_width), jnp.float32)
-
-        return lax.cond(own_row[offset] > 0, one_live_branch, one_dead_branch, None)
-
-    pieces = lax.map(one_group, jnp.arange(row_span // row_count))
-    seller_grad = ring_scatter(pieces.reshape(row_span, embed_width), "market")
-    return (buyer_grad, seller_grad, loss)
-
-
 def shards(buyers, sellers, eligibility, positives):
     blocks = (eligibility > 0).astype(jnp.int32).reshape(NZ, NY, NZ, NY)
     busiest = jnp.max(jnp.sum(blocks, axis=(0, 3)))
     return lax.cond(
         busiest <= SLOTS,
         functools.partial(fused, False, SLOTS),
-        general,
+        functools.partial(fused, True, NZ * NY),
         buyers, sellers, eligibility, positives,
     )
 

time: 78.6 us -> 76.6 us (0.975)
  Pallas kernels: 71.3 us -> 69.8 us
    pallas_call x1, Pallas kernels: 71.3 us -> 69.8 us  [fused(): pl.pallas_call(functools.partial(kernel, dense), out_shape=(jax.ShapeDtyp...]
    unnamed x3 -> x8, local copies, waits for them, and re-layouts: 2.06 us -> 1.42 us
where the time goes in v3:
time: 76.6 us; the launch traced here: 76.2 us
  Pallas kernels  69.8 us (91%)
  between operations  3.12 us (4%)
  other arithmetic  1.56 us (2%)
  local copies, waits for them, and re-layouts  1.51 us (2%)
    pallas_call x1, Pallas kernels, fused(): pl.pallas_call(functools.partial(kernel, dense), out_shape=(jax.ShapeDtyp...  69.8 us

profile of v3, /device:TPU:2, one launch (start us, length us, event | category | flops | bytes accessed | tf_op | source)
XLA Modules:
  0.0 76.2 jit_solution(4547483524632640009)
XLA Ops:
  0.6 0.0 copy-start
  0.6 0.8 %compare_convert_fusion = s32[32,32]{1,0:T(8,128)S(1)} fusion(s32[32,32]{1,0:T(8,128)} %param.8), kind=kLoop, calls=%fused_computation | loop fusion | flops 2048 | bytes 8192 | tf_op jit(solution)/shard_map/reshape | solution.py:694
  1.4 0.1 reshape.21
  1.5 0.0 copy-start.1
  1.5 0.2 reduce_sum.9
  1.7 0.6 reduce_max.9
  2.3 0.0 copy-start.2
  3.0 0.0 copy-done
  3.0 0.0 copy-done.1
  3.0 0.0 copy-done.2
  3.0 70.0 %conditional.1 = (f32[128,512]{1,0:T(8,128)S(1)}, f32[128,512]{1,0:T(8,128)S(1)}, f32[]{:T(128)}) conditional(s32[]{:T(128)} %convert_element_type.4, (s32[128]{0:T(128)S(1)}, f32[128,512]{1,0:T(8,128)S(1)}, f32[128,512]{1,0:T(8,128)}, s32[32,32]{1,0:T(8,128)S(1)}) %tuple.26, (s32[128]{0:T(128)S(1)}, f32[128,512]{1,0:T(8,128)S(1)}, ...), branch_computations={%region_2.0_spmd, %region_3.0_spmd} | conditional | bytes 24 | solution.py:696
  3.2 69.8 %two_tower.1 = (f32[128,512]{1,0:T(8,128)S(1)}, f32[128,512]{1,0:T(8,128)S(1)}, f32[1,128]{1,0:T(1,128)}) custom-call(f32[128,512]{1,0:T(8,128)S(1)} %get-tuple-element.43.buyers_ref, f32[128,512]{1,0:T(8,128)} %get-tuple-element.45.sellers_ref, s32[32,32]{1,0:T(8,128)S(1)} %get-tuple-element.25.elig_ref, s32[1,128]{1,0:T(1,128)S(1)} %bitcast.7), custom_call_target="tpu_custom_call" | custom-call | tf_op jit(solution)/shard_map/cond/branch_1_fun/two_tower/pallas_call | solution.py:675
  73.0 0.7 copy.24
  73.7 0.7 copy.25
Async XLA Ops:
  0.6 2.4 %copy-start = (f32[128,512]{1,0:T(8,128)S(1)}, f32[128,512]{1,0:T(8,128)}, u32[]{:S(2)}) copy-start(f32[128,512]{1,0:T(8,128)} %param.6) | copy-start | bytes 786436
  1.5 1.5 %copy-start.1 = (s32[32,32]{1,0:T(8,128)S(1)}, s32[32,32]{1,0:T(8,128)}, u32[]{:S(2)}) copy-start(s32[32,32]{1,0:T(8,128)} %param.8) | copy-start | bytes 12292
  2.3 0.7 copy-start.2

commit v4 on v3

--- a/solution.py
+++ b/solution.py
@@ -121,17 +121,13 @@
     def core_of(dc):
         return other if dc else c
 
-    for (dz, dc), (dy, dx) in zip(row_steps, col_steps):
-        for peer in (
-            dev(mod(z + dz, NZ), y, x, core_of(dc)),
-            dev(z, mod(y + dy, NY), mod(x + dx, NX), c),
-        ):
-            pl.semaphore_signal(barrier, inc=1, device_id=peer, device_id_type=MESH)
+    for peer in (zdev(1), zdev(-1), ydev(1), ydev(-1), xdev(1), xdev(-1), sibling):
+        pl.semaphore_signal(barrier, inc=1, device_id=peer, device_id_type=MESH)
     b_all[z, c] = buyers_ref[...].astype(BF16)
     s_all[y, x] = sellers_ref[...].astype(BF16)
     own_pos = pos_ref[...] - market * (ROWS * NX * NC)
     pos_f[c] = jnp.broadcast_to(own_pos.astype(F32), (8, ROWS))
-    pl.semaphore_wait(barrier, 30)
+    pl.semaphore_wait(barrier, 7)
 
     names = {}
     landed = set()

time: 76.6 us -> 75.3 us (0.983)
  Pallas kernels: 69.8 us -> 68.7 us
    pallas_call x1, Pallas kernels: 69.8 us -> 68.7 us  [fused(): pl.pallas_call(functools.partial(kernel, dense), out_shape=(jax.ShapeDtyp...]
where the time goes in v4:
time: 75.3 us; the launch traced here: 75.1 us
  Pallas kernels  68.7 us (91%)
  between operations  3.12 us (4%)
  other arithmetic  1.56 us (2%)
  local copies, waits for them, and re-layouts  1.51 us (2%)
    pallas_call x1, Pallas kernels, fused(): pl.pallas_call(functools.partial(kernel, dense), out_shape=(jax.ShapeDtyp...  68.7 us

profile of v4, /device:TPU:2, one launch (start us, length us, event | category | flops | bytes accessed | tf_op | source)
XLA Modules:
  0.0 75.1 jit_solution(10172832027244648470)
XLA Ops:
  0.6 0.0 copy-start
  0.6 0.8 %compare_convert_fusion = s32[32,32]{1,0:T(8,128)S(1)} fusion(s32[32,32]{1,0:T(8,128)} %param.8), kind=kLoop, calls=%fused_computation | loop fusion | flops 2048 | bytes 8192 | tf_op jit(solution)/shard_map/reshape | solution.py:690
  1.4 0.1 reshape.21
  1.5 0.0 copy-start.1
  1.5 0.2 reduce_sum.9
  1.7 0.6 reduce_max.9
  2.3 0.0 copy-start.2
  3.0 0.0 copy-done
  3.0 0.0 copy-done.1
  3.0 0.0 copy-done.2
  3.0 68.9 %conditional.1 = (f32[128,512]{1,0:T(8,128)S(1)}, f32[128,512]{1,0:T(8,128)S(1)}, f32[]{:T(128)}) conditional(s32[]{:T(128)} %convert_element_type.4, (s32[128]{0:T(128)S(1)}, f32[128,512]{1,0:T(8,128)S(1)}, f32[128,512]{1,0:T(8,128)}, s32[32,32]{1,0:T(8,128)S(1)}) %tuple.26, (s32[128]{0:T(128)S(1)}, f32[128,512]{1,0:T(8,128)S(1)}, ...), branch_computations={%region_2.0_spmd, %region_3.0_spmd} | conditional | bytes 24 | solution.py:692
  3.2 68.7 %two_tower.1 = (f32[128,512]{1,0:T(8,128)S(1)}, f32[128,512]{1,0:T(8,128)S(1)}, f32[1,128]{1,0:T(1,128)}) custom-call(f32[128,512]{1,0:T(8,128)S(1)} %get-tuple-element.43.buyers_ref, f32[128,512]{1,0:T(8,128)} %get-tuple-element.45.sellers_ref, s32[32,32]{1,0:T(8,128)S(1)} %get-tuple-element.25.elig_ref, s32[1,128]{1,0:T(1,128)S(1)} %bitcast.7), custom_call_target="tpu_custom_call" | custom-call | tf_op jit(solution)/shard_map/cond/branch_1_fun/two_tower/pallas_call | solution.py:671
  71.9 0.7 copy.24
  72.6 0.7 copy.25
Async XLA Ops:
  0.6 2.4 %copy-start = (f32[128,512]{1,0:T(8,128)S(1)}, f32[128,512]{1,0:T(8,128)}, u32[]{:S(2)}) copy-start(f32[128,512]{1,0:T(8,128)} %param.6) | copy-start | bytes 786436
  1.5 1.5 %copy-start.1 = (s32[32,32]{1,0:T(8,128)S(1)}, s32[32,32]{1,0:T(8,128)}, u32[]{:S(2)}) copy-start(s32[32,32]{1,0:T(8,128)} %param.8) | copy-start | bytes 12292
  2.3 0.7 copy-start.2
